TPU v7x, 256 devices: a whole 4x4x8 slice. The times are simulated.
256 devices in a mesh: leaf: 64 (over y, x, z_lo), panel: 4 (over z_hi, core).
Axes of the slice: x: 4, y: 4, z: 8 (z_hi: 2, z_lo: 4; z = z_hi * 4 + z_lo), core: 2. Of those that a mesh axis runs over, the one named last changes fastest.
Arguments:
- child_front: bfloat16 [16384, 16384], P('leaf', 'panel'), may hold values from -6 to 6
- own_map: int32 [3, 64, 2], P(None, 'leaf'), may hold values from 0 to 1, each once within a row
- cross_map: int32 [3, 64, 2], P(None, 'leaf'), may hold values from 0 to 1, each once within a row
- pivot_inverse: bfloat16 [7, 512, 512], replicated, may hold values from -0.0029296875 to 0.0029296875
Outputs:
- schur: bfloat16 [16384, 16384], P('leaf', 'panel')
Inputs may be any that keep to these rules, and one draw needn't show every extreme that they name: Each own_map[k, d, :] is a permutation of the 2 blocks. Each cross_map[k, d, :] is a permutation of the 2 blocks.
All inputs are finite; a program needn't handle non-finite values.
Results may differ from a plain program's by a relative error of at most 0.0088.
Values may be sent and summed in bfloat16 or wider, within the bound.
A program may use at most 64 MiB of HBM per device.

v0:
```python
import jax
import jax.numpy as jnp
from jax import lax
from jax.sharding import PartitionSpec as P

PANEL = 512
BLOCK = 128


def swapped(block, axis, stride):
    count = lax.axis_size(axis)
    route = []
    for low in range(count):
        high = low | 1 << stride
        if high != low and high < count:
            route += [(low, high), (high, low)]
    return lax.ppermute(block, axis, route)


def spread(block, axis, owner):
    block = jnp.where(lax.axis_index(axis) == owner, block, jnp.zeros_like(block))
    return lax.psum(block, axis)


def extend_add(front_slab, partner, own_index, cross_index, block_count):
    slab_cols = front_slab.shape[1]
    slots = jnp.arange(block_count, dtype=jnp.int32)[None, :]
    own_table = (own_index[:, None] == slots).astype(jnp.bfloat16)
    cross_table = (cross_index[:, None] == slots).astype(jnp.bfloat16)
    own_blocks = front_slab.reshape(block_count, BLOCK, slab_cols)
    cross_blocks = partner.reshape(block_count, BLOCK, slab_cols)
    summed = jnp.einsum("sb,brc->src", own_table, own_blocks, preferred_element_type=jnp.float32)
    summed = summed + jnp.einsum(
        "sb,brc->src", cross_table, cross_blocks, preferred_element_type=jnp.float32
    )
    return summed.reshape(block_count * BLOCK, slab_cols).astype(jnp.bfloat16)


def collect_pivots(own_rows, leaf_index, group_bits):
    buffer = own_rows
    for step_bit in range(group_bits):
        received = swapped(buffer, "leaf", step_bit)
        upper_half = leaf_index >> step_bit & 1 == 1
        buffer = jnp.where(
            upper_half,
            jnp.concatenate([received, buffer], axis=0),
            jnp.concatenate([buffer, received], axis=0),
        )
    return buffer


def top_upper(own_rows, inverse, leaf_index, leaf_bits):
    pivots = collect_pivots(own_rows, leaf_index, leaf_bits)
    product = jnp.dot(inverse, pivots, preferred_element_type=jnp.float32)
    return product.astype(jnp.bfloat16)


def on_device(child_front, own_map, cross_map, pivot_inverse):
    leaf_count = lax.axis_size("leaf")
    leaf_bits = leaf_count.bit_length() - 1
    leaf_index = lax.axis_index("leaf")
    slab_rows = child_front.shape[0]
    block_count = slab_rows // BLOCK
    front_slab = child_front
    offsets = (0, 4, 6)
    for level_index in range(3):
        group_size = leaf_count // 2 ** (2 - level_index)
        group_bits = leaf_bits - 2 + level_index
        share_rows = PANEL // group_size
        partner = swapped(front_slab, "leaf", group_bits - 1)
        parent = extend_add(
            front_slab, partner, own_map[level_index, 0], cross_map[level_index, 0], block_count
        )
        front_number = offsets[level_index] + leaf_index // group_size
        inverse = lax.dynamic_index_in_dim(pivot_inverse, front_number, 0, keepdims=False)
        own_rows = parent[:share_rows]
        if level_index < 2:
            pivots = collect_pivots(own_rows, leaf_index, group_bits)
            upper_rows = jnp.dot(inverse, pivots, preferred_element_type=jnp.float32).astype(
                jnp.bfloat16
            )
        else:
            upper_rows = top_upper(own_rows, inverse, leaf_index, leaf_bits)
        columns = spread(parent[:, :PANEL], "panel", 0)
        reduced = parent.astype(jnp.float32) - jnp.dot(
            columns, upper_rows, preferred_element_type=jnp.float32
        )
        keep_mask = jnp.arange(slab_rows, dtype=jnp.int32)[:, None] >= share_rows
        front_slab = jnp.where(keep_mask, reduced, jnp.zeros_like(reduced)).astype(jnp.bfloat16)
    return front_slab


def solution(mesh):
    placed = (P("leaf", "panel"), P(None, "leaf", None), P(None, "leaf", None), P())
    return jax.shard_map(
        on_device, mesh=mesh, in_specs=placed, out_specs=P("leaf", "panel"), check_vma=False
    )
```

profile of v0, /device:TPU:1, one launch (start us, length us, event | category | flops | bytes accessed | tf_op | source)
XLA Modules:
  0.0 538.7 jit_solution(12298717727944464459)
XLA Ops:
  6.5 3.6 collective-permute-start
  12.1 4.0 fusion.34
  16.2 38.6 %collective-permute-done = bf16[256,4096]{1,0:T(8,128)(2,1)S(1)} collective-permute-done((bf16[256,4096]{1,0:T(8,128)(2,1)}, bf16[256,4096]{1,0:T(8,128)(2,1)S(1)}, u32[]{:S(2)}, u32[]{:S(2)}) %collective-permute-start) | collective-permute-done | bytes 2097184 | tf_op jit(solution)/shard_map/ppermute | solution.py:17
  61.7 5.1 collective-permute-done.1
  69.9 22.6 %collective-permute-done.2 = bf16[64,4096]{1,0:T(8,128)(2,1)} collective-permute-done((bf16[64,4096]{1,0:T(8,128)(2,1)S(1)}, bf16[64,4096]{1,0:T(8,128)(2,1)}, u32[]{:S(2)}, u32[]{:S(2)}) %collective-permute-start.2) | collective-permute-done | bytes 524320 | tf_op jit(solution)/shard_map/ppermute | solution.py:17
  95.7 22.0 %collective-permute-done.3 = bf16[128,4096]{1,0:T(8,128)(2,1)} collective-permute-done((bf16[128,4096]{1,0:T(8,128)(2,1)S(1)}, bf16[128,4096]{1,0:T(8,128)(2,1)}, u32[]{:S(2)}, u32[]{:S(2)}) %collective-permute-start.3) | collective-permute-done | bytes 1048608 | tf_op jit(solution)/shard_map/ppermute | solution.py:17
  124.7 57.9 %all-reduce.4.cloned.1.call-done = bf16[256,512]{1,0:T(8,128)(2,1)} async-done(((bf16[256,512]{1,0:T(8,128)(2,1)}), bf16[256,512]{1,0:T(8,128)(2,1)}) %all-reduce.4.cloned.1.call-update) | async-done | bytes 262160 | tf_op jit(solution)/shard_map/psum | solution.py:22
  182.6 7.2 %fusion.5 = bf16[256,4096]{1,0:T(8,128)(2,1)} fusion(bf16[256,512]{1,0:T(8,128)(2,1)} %all-reduce.4.cloned.1.call-done, bf16[256,4096]{1,0:T(8,128)(2,1)S(1)} %bitcast.44, bf16[256,4096]{1,0:T(8,128)(2,1)} %maximum_select_fusion.12, bf16[256,4096]{1,0:T(8,128)(2,1)} %collective-permute-done.4, pred[]{:T(512)S(6)} %eq.139, ...), kind=kOutput, calls=%fused_computation.14 | convolution fusion | flops 3246391296 | bytes 9175301 | tf_op jit(solution)/shard_map/dot_general | solution.py:85
  190.5 4.1 fusion.31
  194.5 43.1 %collective-permute-done.5 = bf16[256,4096]{1,0:T(8,128)(2,1)S(1)} collective-permute-done((bf16[256,4096]{1,0:T(8,128)(2,1)}, bf16[256,4096]{1,0:T(8,128)(2,1)S(1)}, u32[]{:S(2)}, u32[]{:S(2)}) %collective-permute-start.5) | collective-permute-done | bytes 2097184 | tf_op jit(solution)/shard_map/ppermute | solution.py:17
  242.0 4.5 collective-permute-done.6
  246.7 14.7 %collective-permute-done.7 = bf16[32,4096]{1,0:T(8,128)(2,1)S(1)} collective-permute-done((bf16[32,4096]{1,0:T(8,128)(2,1)S(1)}, bf16[32,4096]{1,0:T(8,128)(2,1)S(1)}, u32[]{:S(2)}, u32[]{:S(2)}) %collective-permute-start.7) | collective-permute-done | bytes 262176 | tf_op jit(solution)/shard_map/ppermute | solution.py:17
  261.6 13.0 %collective-permute-done.8 = bf16[64,4096]{1,0:T(8,128)(2,1)S(1)} collective-permute-done((bf16[64,4096]{1,0:T(8,128)(2,1)S(1)}, bf16[64,4096]{1,0:T(8,128)(2,1)S(1)}, u32[]{:S(2)}, u32[]{:S(2)}) %collective-permute-start.8) | collective-permute-done | bytes 524320 | tf_op jit(solution)/shard_map/ppermute | solution.py:17
  275.9 23.7 %collective-permute-done.9 = bf16[128,4096]{1,0:T(8,128)(2,1)S(1)} collective-permute-done((bf16[128,4096]{1,0:T(8,128)(2,1)S(1)}, bf16[128,4096]{1,0:T(8,128)(2,1)S(1)}, u32[]{:S(2)}, u32[]{:S(2)}) %collective-permute-start.9) | collective-permute-done | bytes 1048608 | tf_op jit(solution)/shard_map/ppermute | solution.py:17
  302.5 52.4 %all-reduce.6.cloned.1.call-done = bf16[256,512]{1,0:T(8,128)(2,1)} async-done(((bf16[256,512]{1,0:T(8,128)(2,1)}), bf16[256,512]{1,0:T(8,128)(2,1)}) %all-reduce.6.cloned.1.call-update) | async-done | bytes 262160 | tf_op jit(solution)/shard_map/psum | solution.py:22
  354.9 7.2 %fusion.4 = bf16[256,4096]{1,0:T(8,128)(2,1)} fusion(bf16[256,512]{1,0:T(8,128)(2,1)} %all-reduce.6.cloned.1.call-done, bf16[256,4096]{1,0:T(8,128)(2,1)S(1)} %bitcast.47, bf16[256,4096]{1,0:T(8,128)(2,1)} %maximum_select_fusion.13, bf16[256,4096]{1,0:T(8,128)(2,1)} %collective-permute-done.10, pred[]{:T(512)S(6)} %eq.147, ...), kind=kOutput, calls=%fused_computation.13 | convolution fusion | flops 3246391296 | bytes 9175301 | tf_op jit(solution)/shard_map/dot_general | solution.py:85
  364.3 4.1 fusion.28
  368.3 42.9 %collective-permute-done.11 = bf16[256,4096]{1,0:T(8,128)(2,1)S(1)} collective-permute-done((bf16[256,4096]{1,0:T(8,128)(2,1)}, bf16[256,4096]{1,0:T(8,128)(2,1)S(1)}, u32[]{:S(2)}, u32[]{:S(2)}) %collective-permute-start.11) | collective-permute-done | bytes 2097184 | tf_op jit(solution)/shard_map/ppermute | solution.py:17
  418.9 8.4 %collective-permute-done.13 = bf16[16,4096]{1,0:T(8,128)(2,1)S(1)} collective-permute-done((bf16[16,4096]{1,0:T(8,128)(2,1)S(1)}, bf16[16,4096]{1,0:T(8,128)(2,1)S(1)}, u32[]{:S(2)}, u32[]{:S(2)}) %collective-permute-start.13) | collective-permute-done | bytes 131104 | tf_op jit(solution)/shard_map/ppermute | solution.py:17
  427.5 6.9 %collective-permute-done.14 = bf16[32,4096]{1,0:T(8,128)(2,1)S(1)} collective-permute-done((bf16[32,4096]{1,0:T(8,128)(2,1)S(1)}, bf16[32,4096]{1,0:T(8,128)(2,1)S(1)}, u32[]{:S(2)}, u32[]{:S(2)}) %collective-permute-start.14) | collective-permute-done | bytes 262176 | tf_op jit(solution)/shard_map/ppermute | solution.py:17
  434.9 12.7 %collective-permute-done.15 = bf16[64,4096]{1,0:T(8,128)(2,1)S(1)} collective-permute-done((bf16[64,4096]{1,0:T(8,128)(2,1)S(1)}, bf16[64,4096]{1,0:T(8,128)(2,1)S(1)}, u32[]{:S(2)}, u32[]{:S(2)}) %collective-permute-start.15) | collective-permute-done | bytes 524320 | tf_op jit(solution)/shard_map/ppermute | solution.py:17
  448.0 21.9 %collective-permute-done.16 = bf16[128,4096]{1,0:T(8,128)(2,1)S(1)} collective-permute-done((bf16[128,4096]{1,0:T(8,128)(2,1)S(1)}, bf16[128,4096]{1,0:T(8,128)(2,1)S(1)}, u32[]{:S(2)}, u32[]{:S(2)}) %collective-permute-start.16) | collective-permute-done | bytes 1048608 | tf_op jit(solution)/shard_map/ppermute | solution.py:17
  472.6 52.5 %all-reduce.8.cloned.1.call-done = bf16[256,512]{1,0:T(8,128)(2,1)} async-done(((bf16[256,512]{1,0:T(8,128)(2,1)}), bf16[256,512]{1,0:T(8,128)(2,1)}) %all-reduce.8.cloned.1.call-update) | async-done | bytes 262160 | tf_op jit(solution)/shard_map/psum | solution.py:22
  525.1 7.1 %fusion.3 = bf16[256,4096]{1,0:T(8,128)(2,1)} fusion(bf16[256,512]{1,0:T(8,128)(2,1)} %all-reduce.8.cloned.1.call-done, bf16[256,4096]{1,0:T(8,128)(2,1)S(1)} %bitcast.50, bf16[256,4096]{1,0:T(8,128)(2,1)} %maximum_select_fusion.14, bf16[256,4096]{1,0:T(8,128)(2,1)} %collective-permute-done.17, pred[]{:T(512)S(6)} %eq.152, ...), kind=kOutput, calls=%fused_computation.12 | convolution fusion | flops 3246391296 | bytes 9175301 | tf_op jit(solution)/shard_map/dot_general | solution.py:85
  (58 shorter events, 45.3 us)
Async XLA Ops:
  6.5 176.1 %all-reduce.4.cloned.1.call-start = ((), (), s32[]{:S(2)}) async-start(), calls=%async_computation | async-start | bytes 524288 | tf_op jit(solution)/shard_map/psum | solution.py:22
  6.5 48.2 %collective-permute-start = (bf16[256,4096]{1,0:T(8,128)(2,1)}, bf16[256,4096]{1,0:T(8,128)(2,1)S(1)}, u32[]{:S(2)}, u32[]{:S(2)}) collective-permute-start(bf16[256,4096]{1,0:T(8,128)(2,1)} %param.4), channel_id=1, source_target_pairs={{0,32},{32,0},{4,36},{36,4},{8,40},{40,8},{12,44},{44,12},{16,48},... | collective-permute-start | bytes 6291464 | tf_op jit(solution)/shard_map/ppermute | solution.py:17
  59.1 7.7 %collective-permute-start.1 = (bf16[32,4096]{1,0:T(8,128)(2,1)S(1)}, bf16[32,4096]{1,0:T(8,128)(2,1)S(1)}, u32[]{:S(2)}, u32[]{:S(2)}) collective-permute-start(bf16[32,4096]{1,0:T(8,128)(2,1)S(1)} %slice.49), channel_id=1, source_target_pairs={{0,4},{4,0},{8,12},{12,8},{16,20},{20,16},{24,28},{28,24},{32,36},... | collective-permute-start | bytes 786440 | tf_op jit(solution)/shard_map/ppermute | solution.py:17
  66.9 3.0 copy-start
  66.9 25.6 %collective-permute-start.2 = (bf16[64,4096]{1,0:T(8,128)(2,1)S(1)}, bf16[64,4096]{1,0:T(8,128)(2,1)}, u32[]{:S(2)}, u32[]{:S(2)}) collective-permute-start(bf16[64,4096]{1,0:T(8,128)(2,1)S(1)} %maximum_select_fusion.18), channel_id=1, source_target_pairs={{0,8},{8,0},{4,12},{12,4},{16,24},{24,16},{20,28},{28,20},{32,40},... | collective-permute-start | bytes 1572872 | tf_op jit(solution)/shard_map/ppermute | solution.py:17
  94.4 23.3 %collective-permute-start.3 = (bf16[128,4096]{1,0:T(8,128)(2,1)S(1)}, bf16[128,4096]{1,0:T(8,128)(2,1)}, u32[]{:S(2)}, u32[]{:S(2)}) collective-permute-start(bf16[128,4096]{1,0:T(8,128)(2,1)S(1)} %maximum_select_fusion.15), channel_id=1, source_target_pairs={{0,16},{16,0},{4,20},{20,4},{8,24},{24,8},{12,28},{28,12},{32,48},... | collective-permute-start | bytes 3145736 | tf_op jit(solution)/shard_map/ppermute | solution.py:17
  121.1 61.5 %collective-permute-start.4 = (bf16[256,4096]{1,0:T(8,128)(2,1)}, bf16[256,4096]{1,0:T(8,128)(2,1)}, u32[]{:S(2)}, u32[]{:S(2)}) collective-permute-start(bf16[256,4096]{1,0:T(8,128)(2,1)} %maximum_select_fusion.12), channel_id=1, source_target_pairs={{0,32},{32,0},{4,36},{36,4},{8,40},{40,8},{12,44},{44,12},{16,48},... | collective-permute-start | bytes 6291464 | tf_op jit(solution)/shard_map/ppermute | solution.py:17
  124.6 230.2 %all-reduce.6.cloned.1.call-start = ((), (), s32[]{:S(2)}) async-start(), calls=%async_computation.1 | async-start | bytes 524288 | tf_op jit(solution)/shard_map/psum | solution.py:22
  189.9 47.7 %collective-permute-start.5 = (bf16[256,4096]{1,0:T(8,128)(2,1)}, bf16[256,4096]{1,0:T(8,128)(2,1)S(1)}, u32[]{:S(2)}, u32[]{:S(2)}) collective-permute-start(bf16[256,4096]{1,0:T(8,128)(2,1)} %fusion.5), channel_id=1, source_target_pairs={{0,64},{64,0},{4,68},{68,4},{8,72},{72,8},{12,76},{76,12},{16,80},... | collective-permute-start | bytes 6291464 | tf_op jit(solution)/shard_map/ppermute | solution.py:17
  241.9 4.6 collective-permute-start.6
  246.6 14.8 %collective-permute-start.7 = (bf16[32,4096]{1,0:T(8,128)(2,1)S(1)}, bf16[32,4096]{1,0:T(8,128)(2,1)S(1)}, u32[]{:S(2)}, u32[]{:S(2)}) collective-permute-start(bf16[32,4096]{1,0:T(8,128)(2,1)S(1)} %maximum_select_fusion.21), channel_id=1, source_target_pairs={{0,8},{8,0},{4,12},{12,4},{16,24},{24,16},{20,28},{28,20},{32,40},... | collective-permute-start | bytes 786440 | tf_op jit(solution)/shard_map/ppermute | solution.py:17
  261.5 13.1 %collective-permute-start.8 = (bf16[64,4096]{1,0:T(8,128)(2,1)S(1)}, bf16[64,4096]{1,0:T(8,128)(2,1)S(1)}, u32[]{:S(2)}, u32[]{:S(2)}) collective-permute-start(bf16[64,4096]{1,0:T(8,128)(2,1)S(1)} %maximum_select_fusion.19), channel_id=1, source_target_pairs={{0,16},{16,0},{4,20},{20,4},{8,24},{24,8},{12,28},{28,12},{32,48},... | collective-permute-start | bytes 1572872 | tf_op jit(solution)/shard_map/ppermute | solution.py:17
  274.8 24.9 %collective-permute-start.9 = (bf16[128,4096]{1,0:T(8,128)(2,1)S(1)}, bf16[128,4096]{1,0:T(8,128)(2,1)S(1)}, u32[]{:S(2)}, u32[]{:S(2)}) collective-permute-start(bf16[128,4096]{1,0:T(8,128)(2,1)S(1)} %maximum_select_fusion.16), channel_id=1, source_target_pairs={{0,32},{32,0},{4,36},{36,4},{8,40},{40,8},{12,44},{44,12},{16,48},... | collective-permute-start | bytes 3145736 | tf_op jit(solution)/shard_map/ppermute | solution.py:17
  301.6 53.2 %collective-permute-start.10 = (bf16[256,4096]{1,0:T(8,128)(2,1)}, bf16[256,4096]{1,0:T(8,128)(2,1)}, u32[]{:S(2)}, u32[]{:S(2)}) collective-permute-start(bf16[256,4096]{1,0:T(8,128)(2,1)} %maximum_select_fusion.13), channel_id=1, source_target_pairs={{0,64},{64,0},{4,68},{68,4},{8,72},{72,8},{12,76},{76,12},{16,80},... | collective-permute-start | bytes 6291464 | tf_op jit(solution)/shard_map/ppermute | solution.py:17
  302.4 222.7 %all-reduce.8.cloned.1.call-start = ((), (), s32[]{:S(2)}) async-start(), calls=%async_computation.2 | async-start | bytes 524288 | tf_op jit(solution)/shard_map/psum | solution.py:22
  362.0 49.2 %collective-permute-start.11 = (bf16[256,4096]{1,0:T(8,128)(2,1)}, bf16[256,4096]{1,0:T(8,128)(2,1)S(1)}, u32[]{:S(2)}, u32[]{:S(2)}) collective-permute-start(bf16[256,4096]{1,0:T(8,128)(2,1)} %fusion.4), channel_id=1, source_target_pairs={{0,128},{128,0},{4,132},{132,4},{8,136},{136,8},{12,140},{140,12},... | collective-permute-start | bytes 6291464 | tf_op jit(solution)/shard_map/ppermute | solution.py:17
  415.6 3.2 collective-permute-start.12
  418.8 8.5 %collective-permute-start.13 = (bf16[16,4096]{1,0:T(8,128)(2,1)S(1)}, bf16[16,4096]{1,0:T(8,128)(2,1)S(1)}, u32[]{:S(2)}, u32[]{:S(2)}) collective-permute-start(bf16[16,4096]{1,0:T(8,128)(2,1)S(1)} %maximum_select_fusion.23), channel_id=1, source_target_pairs={{0,8},{8,0},{4,12},{12,4},{16,24},{24,16},{20,28},{28,20},{32,40},... | collective-permute-start | bytes 393224 | tf_op jit(solution)/shard_map/ppermute | solution.py:17
  427.4 7.0 %collective-permute-start.14 = (bf16[32,4096]{1,0:T(8,128)(2,1)S(1)}, bf16[32,4096]{1,0:T(8,128)(2,1)S(1)}, u32[]{:S(2)}, u32[]{:S(2)}) collective-permute-start(bf16[32,4096]{1,0:T(8,128)(2,1)S(1)} %maximum_select_fusion.22), channel_id=1, source_target_pairs={{0,16},{16,0},{4,20},{20,4},{8,24},{24,8},{12,28},{28,12},{32,48},... | collective-permute-start | bytes 786440 | tf_op jit(solution)/shard_map/ppermute | solution.py:17
  434.4 13.2 %collective-permute-start.15 = (bf16[64,4096]{1,0:T(8,128)(2,1)S(1)}, bf16[64,4096]{1,0:T(8,128)(2,1)S(1)}, u32[]{:S(2)}, u32[]{:S(2)}) collective-permute-start(bf16[64,4096]{1,0:T(8,128)(2,1)S(1)} %maximum_select_fusion.20), channel_id=1, source_target_pairs={{0,32},{32,0},{4,36},{36,4},{8,40},{40,8},{12,44},{44,12},{16,48},... | collective-permute-start | bytes 1572872 | tf_op jit(solution)/shard_map/ppermute | solution.py:17
  447.9 22.0 %collective-permute-start.16 = (bf16[128,4096]{1,0:T(8,128)(2,1)S(1)}, bf16[128,4096]{1,0:T(8,128)(2,1)S(1)}, u32[]{:S(2)}, u32[]{:S(2)}) collective-permute-start(bf16[128,4096]{1,0:T(8,128)(2,1)S(1)} %maximum_select_fusion.17), channel_id=1, source_target_pairs={{0,64},{64,0},{4,68},{68,4},{8,72},{72,8},{12,76},{76,12},{16,80},... | collective-permute-start | bytes 3145736 | tf_op jit(solution)/shard_map/ppermute | solution.py:17
  471.8 53.2 %collective-permute-start.17 = (bf16[256,4096]{1,0:T(8,128)(2,1)}, bf16[256,4096]{1,0:T(8,128)(2,1)}, u32[]{:S(2)}, u32[]{:S(2)}) collective-permute-start(bf16[256,4096]{1,0:T(8,128)(2,1)} %maximum_select_fusion.14), channel_id=1, source_target_pairs={{0,128},{128,0},{4,132},{132,4},{8,136},{136,8},{12,140},{140,12},... | collective-permute-start | bytes 6291464 | tf_op jit(solution)/shard_map/ppermute | solution.py:17
Sparse Core Ops, SparseCore 0:
  124.8 57.8 all-reduce.3
  302.5 52.3 all-reduce.5
  472.7 52.3 all-reduce.7
where the time goes:
time: 539 us
  waiting for transfers between devices  446 us (83%)
  matrix products  42.6 us (8%)
  starting transfers between devices  18.4 us (3%)
  between operations  13.4 us (2%)
  other arithmetic  12.3 us (2%)
  local copies, waits for them, and re-layouts  6.04 us (1%)
    ppermute x18, waiting for transfers between devices, swapped(): return lax.ppermute(block, axis, route)  283 us
    psum x3, waiting for transfers between devices, spread(): return lax.psum(block, axis)  163 us
    dot_general x3, matrix products, on_device(): jnp.dot(columns, upper_rows, preferred_element_type=jnp.float32)  21.5 us
    ppermute x18, starting transfers between devices, swapped(): return lax.ppermute(block, axis, route)  18.3 us
    dot_general x3, matrix products, extend_add(): jnp.einsum('sb,brc->src', own_table, own_blocks, preferred_element_type=j...  12.1 us
  transfers between devices with their start and end apart: 21, of which 18 were waited for; matrix products, arithmetic and copies ran while one was open for 3% of the time, Pallas kernels for 0%

commit v1 on v0

v1 whole, which is shorter than its diff:
```python
import functools

import jax
import jax.numpy as jnp
from jax import lax
from jax.experimental import pallas as pl
from jax.experimental.pallas import tpu as pltpu
from jax.sharding import PartitionSpec as P

PANEL = 512
BLOCK = 128
WIDTH = 256
MESH = pl.DeviceIdType.MESH
F32 = jnp.float32
BF16 = jnp.bfloat16


def multiple(value, of):
    return pl.multiple_of(value, of)


def kernel(
    child, maps, inverse, out,
    front, parent, pfront, pparent, inv, map_buf, map_tab,
    piv0, piv1, piv2, ppiv0, ppiv1, upper, pupper0, pupper1,
    map_send, map_recv, a2a_send, a2a_recv, first_send, first_recv,
    pan_send, pan_recv, fwd_send, fwd_recv, piv0_send, piv0_recv,
    piv1_send, piv1_recv, piv2_send, piv2_recv, pp0_send, pp0_recv,
    pp1_send, pp1_recv, up0_send, up0_recv, up0f_send, up0f_recv,
    up1_send, up1_recv, up1f_send, up1f_recv, out_send, out_recv, local_sem,
):
    leaf = lax.axis_index("leaf")
    panel = lax.axis_index("panel")
    g, r = leaf // 4, leaf % 4
    y, x = g // 4, g % 4
    core = panel % 2
    mate = panel + 1 - 2 * core

    def at(dy, dx):
        return ((y + dy) % 4) * 4 + (x + dx) % 4

    def each_peer(stage, visit):
        if stage == 0:
            @pl.loop(1, 4)
            def _(i):
                visit(0, i)
        elif stage == 1:
            @pl.loop(0, 4)
            def _(i):
                visit(1, i)
                visit(3, i)
        else:
            @pl.loop(0, 4)
            def _(i):
                visit(2, i)

    def remote(src, dst, send, recv, to_leaf, to_panel):
        return pltpu.make_async_remote_copy(
            src_ref=src, dst_ref=dst, send_sem=send, recv_sem=recv,
            device_id=(to_leaf, to_panel), device_id_type=MESH,
        )

    barrier = pltpu.get_barrier_semaphore()

    def greet(dy, dx):
        pl.semaphore_signal(barrier, inc=1, device_id=(at(dy, dx) * 4 + r, panel), device_id_type=MESH)

    for stage in range(3):
        each_peer(stage, greet)

    @pl.loop(1, 4)
    def _(i):
        pl.semaphore_signal(barrier, inc=1, device_id=(g * 4 + (r + i) % 4, panel), device_id_type=MESH)
        pl.semaphore_signal(barrier, inc=1, device_id=(leaf, (panel + i) % 4), device_id_type=MESH)

    def columns(which):
        return pl.ds(multiple(which * WIDTH, WIDTH), WIDTH)

    own_copy = pltpu.make_async_copy(child.at[:, :, columns(g)], front.at[g], local_sem.at[0])
    own_copy.start()
    inv_copy = pltpu.make_async_copy(inverse, inv, local_sem.at[1])
    inv_copy.start()
    map_copy = pltpu.make_async_copy(maps, map_buf.at[g], local_sem.at[2])
    map_copy.start()
    pl.semaphore_wait(barrier, 21)

    def first_copy(half, to_panel, index):
        return remote(
            child.at[half, :, pl.ds(0, PANEL)], pfront.at[g, half],
            first_send.at[index], first_recv.at[0], leaf, to_panel,
        )

    first_own = pltpu.make_async_copy(child.at[0, :, pl.ds(0, PANEL)], pfront.at[g, 0], local_sem.at[3])

    @pl.when(panel == 0)
    def _():
        first_copy(0, 2, 1).start()
        first_copy(1, 3, 2).start()
        first_copy(1, 1, 0).start()
        first_own.start()

    def map_of(slab, to):
        return remote(maps, map_buf.at[slab], map_send.at[to], map_recv.at[slab], to * 4 + r, panel)

    def a2a_of(slab, to):
        return remote(child.at[:, :, columns(to)], front.at[slab], a2a_send.at[to], a2a_recv.at[slab], to * 4 + r, panel)

    def pan_of(slab, to):
        return remote(pfront.at[slab, core], pfront.at[slab, core], pan_send.at[to], pan_recv.at[slab], to * 4 + r, panel)

    def send_child(dy, dx):
        to = at(dy, dx)
        map_of(g, to).start()
        a2a_of(g, to).start()

    def send_panel(dy, dx):
        pan_of(g, at(dy, dx)).start()

    each_peer(0, send_child)

    @pl.when(panel == 0)
    def _():
        first_own.wait()

    @pl.when(panel != 0)
    def _():
        first_copy(core, panel, 0).wait_recv()

    each_peer(0, send_panel)
    each_peer(1, send_child)
    each_peer(1, send_panel)
    each_peer(2, send_child)
    each_peer(2, send_panel)

    own_copy.wait()
    map_copy.wait()

    def take_map(dy, dx):
        map_of(at(dy, dx), g).wait_recv()

    for stage in range(3):
        each_peer(stage, take_map)
    to_smem = pltpu.make_async_copy(map_buf, map_tab, local_sem.at[2])
    to_smem.start()
    to_smem.wait()

    def extend(src, dst, level, a, b):
        width = src.shape[3]
        for mine, other in ((a, b), (b, a)):
            for slot in range(2):
                from_own = map_tab[mine, level, slot] == 0
                from_cross = map_tab[mine, level, 2 + slot] == 0
                for low in range(0, BLOCK, 32):
                    for left in range(0, width, WIDTH):
                        part = (pl.ds(low, 32), pl.ds(left, WIDTH))
                        kept = jnp.where(from_own, src[(mine, 0) + part], src[(mine, 1) + part])
                        moved = jnp.where(from_cross, src[(other, 0) + part], src[(other, 1) + part])
                        dst[(mine, slot) + part] = (kept.astype(F32) + moved.astype(F32)).astype(BF16)

    def subtract(src, dst, factor, top, slab, rows):
        width = src.shape[3]
        left = pparent[slab].reshape(2 * BLOCK, PANEL)
        keep = lax.broadcasted_iota(jnp.int32, (2 * BLOCK, WIDTH), 0) >= rows
        for low in range(0, width, WIDTH):
            part = pl.ds(low, WIDTH)
            product = jnp.dot(left, factor[top, :, part], preferred_element_type=F32)
            start = src[slab, :, :, part].reshape(2 * BLOCK, WIDTH).astype(F32)
            reduced = jnp.where(keep, start - product, 0.0).astype(BF16)
            dst[slab, :, :, part] = reduced.reshape(2, BLOCK, WIDTH)

    def piv0_of(f, owner, to):
        slabs = pl.ds(f * 4, 4)
        return remote(
            parent.at[slabs, 0, pl.ds(0, 32), :], piv0.at[slabs, owner],
            piv0_send.at[f, to], piv0_recv.at[f, owner], g * 4 + to, panel,
        )

    def fwd_of(f, half):
        part = pfront.at[pl.ds(f * 4, 4), half]
        return remote(part, part, fwd_send.at[f], fwd_recv.at[f], leaf, mate)

    def open_front(f):
        fwd_of(f, core).start()

        @pl.loop(0, 2)
        def _(j):
            extend(front, parent, 0, f * 4 + j, f * 4 + j + 2)

        @pl.loop(1, 4)
        def _(i):
            piv0_of(f, r, (r + i) % 4).start()

        @pl.loop(0, 4)
        def _(j):
            piv0[f * 4 + j, r] = parent[f * 4 + j, 0, 0:32, :]

    def open_panel(f):
        fwd_of(f, 1 - core).wait_recv()

        @pl.loop(0, 2)
        def _(j):
            extend(pfront, pparent, 0, f * 4 + j, f * 4 + j + 2)

    def take_slab(dy, dx):
        a2a_of(at(dy, dx), g).wait_recv()
        pan_of(at(dy, dx), g).wait_recv()

    piece = pl.ds(multiple(x * BLOCK, BLOCK), BLOCK)

    def pp0_of(owner, to):
        return remote(
            pparent.at[pl.ds(y * 4, 4), 0, pl.ds(0, 32), piece], ppiv0.at[:, owner],
            pp0_send.at[to], pp0_recv.at[owner], g * 4 + to, panel,
        )

    def up0_of(slab, to):
        part = pupper0.at[
            slab // 4, pl.ds(multiple(core * 256, 256), 256), pl.ds(multiple(slab % 4 * BLOCK, BLOCK), BLOCK)
        ]
        return remote(part, part, up0_send.at[to], up0_recv.at[slab], to * 4 + r, panel)

    def up0f_of(f, half):
        part = pupper0.at[f, pl.ds(multiple(half * 256, 256), 256), :]
        return remote(part, part, up0f_send.at[f], up0f_recv.at[f], leaf, mate)

    each_peer(0, take_slab)
    open_front(y)
    open_panel(y)

    @pl.loop(1, 4)
    def _(i):
        pp0_of(r, (r + i) % 4).start()

    @pl.loop(0, 4)
    def _(j):
        ppiv0[j, r] = pparent[y * 4 + j, 0, 0:32, piece]

    inv_copy.wait()

    @pl.loop(1, 4)
    def _(i):
        pp0_of((r + i) % 4, r).wait_recv()

    half0 = pl.ds(multiple(core * 256, 256), 256)
    pupper0[y, half0, piece] = jnp.dot(
        inv[y, half0, :], ppiv0[...].reshape(PANEL, BLOCK), preferred_element_type=F32
    ).astype(BF16)
    for stage in range(3):
        each_peer(stage, lambda dy, dx: up0_of(g, at(dy, dx)).start())

    each_peer(1, take_slab)
    open_front((y + 1) % 4)
    open_front((y + 3) % 4)
    open_panel((y + 1) % 4)
    open_panel((y + 3) % 4)
    each_peer(2, take_slab)
    open_front((y + 2) % 4)
    open_panel((y + 2) % 4)

    each_peer(0, lambda dy, dx: up0_of(at(dy, dx), g).wait_recv())
    up0f_of(y, core).start()
    each_peer(1, lambda dy, dx: up0_of(at(dy, dx), g).wait_recv())
    up0f_of((y + 1) % 4, core).start()
    up0f_of((y + 3) % 4, core).start()
    each_peer(2, lambda dy, dx: up0_of(at(dy, dx), g).wait_recv())
    up0f_of((y + 2) % 4, core).start()

    @pl.when(panel == 0)
    def _():
        for index in range(3):
            first_copy(0, 1, index).wait_send()

    for stage in range(3):
        each_peer(stage, lambda dy, dx: pan_of(g, at(dy, dx)).wait_send())

    @pl.loop(0, 4)
    def _(f):
        fwd_of(f, core).wait_send()

    @pl.loop(0, 4)
    def _(f):
        up0f_of(f, 1 - core).wait_recv()

        @pl.loop(0, 4)
        def _(j):
            subtract(pparent, pfront, pupper0, f, f * 4 + j, 32)

    @pl.loop(0, 4)
    def _(f):
        @pl.loop(1, 4)
        def _(i):
            piv0_of(f, (r + i) % 4, r).wait_recv()

        upper[f] = jnp.dot(
            inv[f], piv0[pl.ds(f * 4, 4)].reshape(PANEL, WIDTH), preferred_element_type=F32
        ).astype(BF16)

        @pl.loop(0, 4)
        def _(j):
            subtract(parent, front, upper, f, f * 4 + j, 32)

    @pl.loop(0, 4)
    def _(f):
        @pl.loop(1, 4)
        def _(i):
            piv0_of(f, r, (r + i) % 4).wait_send()

    @pl.loop(1, 4)
    def _(i):
        pp0_of(r, (r + i) % 4).wait_send()

    def piv1_of(owner, to):
        return remote(
            parent.at[:, 0, pl.ds(0, 16), :], piv1.at[:, owner],
            piv1_send.at[to], piv1_recv.at[owner], g * 4 + to, panel,
        )

    def pp1_of(owner, to):
        return remote(
            pparent.at[pl.ds(y // 2 * 8, 8), 0, pl.ds(0, 16), piece], ppiv1.at[:, owner],
            pp1_send.at[to], pp1_recv.at[owner], g * 4 + to, panel,
        )

    def up1_of(slab, to):
        part = pupper1.at[
            slab // 8,
            pl.ds(multiple(core * 256 + slab // 4 % 2 * BLOCK, BLOCK), BLOCK),
            pl.ds(multiple(slab % 4 * BLOCK, BLOCK), BLOCK),
        ]
        return remote(part, part, up1_send.at[to], up1_recv.at[slab], to * 4 + r, panel)

    def up1f_of(f, half):
        part = pupper1.at[f, pl.ds(multiple(half * 256, 256), 256), :]
        return remote(part, part, up1f_send.at[f], up1f_recv.at[f], leaf, mate)

    @pl.loop(0, 2)
    def _(f):
        @pl.loop(0, 4)
        def _(j):
            extend(front, parent, 1, f * 8 + j, f * 8 + j + 4)

    @pl.loop(1, 4)
    def _(i):
        piv1_of(r, (r + i) % 4).start()

    @pl.loop(0, 16)
    def _(j):
        piv1[j, r] = parent[j, 0, 0:16, :]

    @pl.loop(0, 2)
    def _(f):
        @pl.loop(0, 4)
        def _(j):
            extend(pfront, pparent, 1, f * 8 + j, f * 8 + j + 4)

    @pl.loop(1, 4)
    def _(i):
        pp1_of(r, (r + i) % 4).start()

    @pl.loop(0, 8)
    def _(j):
        ppiv1[j, r] = pparent[y // 2 * 8 + j, 0, 0:16, piece]

    @pl.loop(1, 4)
    def _(i):
        pp1_of((r + i) % 4, r).wait_recv()

    quarter = pl.ds(multiple(core * 256 + y % 2 * BLOCK, BLOCK), BLOCK)
    pupper1[y // 2, quarter, piece] = jnp.dot(
        inv[4 + y // 2, quarter, :], ppiv1[...].reshape(PANEL, BLOCK), preferred_element_type=F32
    ).astype(BF16)
    for stage in range(3):
        each_peer(stage, lambda dy, dx: up1_of(g, at(dy, dx)).start())

    @pl.loop(1, 4)
    def _(i):
        piv1_of((r + i) % 4, r).wait_recv()

    @pl.loop(0, 2)
    def _(f):
        upper[f] = jnp.dot(
            inv[4 + f], piv1[pl.ds(f * 8, 8)].reshape(PANEL, WIDTH), preferred_element_type=F32
        ).astype(BF16)

        @pl.loop(0, 8)
        def _(j):
            subtract(parent, front, upper, f, f * 8 + j, 16)

    @pl.loop(1, 4)
    def _(i):
        piv1_of(r, (r + i) % 4).wait_send()
        pp1_of(r, (r + i) % 4).wait_send()

    def piv2_of(owner, to):
        return remote(
            piv2.at[:, owner], piv2.at[:, owner],
            piv2_send.at[to], piv2_recv.at[owner], g * 4 + to, panel,
        )

    @pl.loop(0, 8)
    def _(j):
        extend(front, parent, 2, j, j + 8)

    @pl.loop(0, 16)
    def _(j):
        piv2[j, r] = parent[j, 0, 0:16, :].astype(F32)[0:8]

    @pl.loop(1, 4)
    def _(i):
        piv2_of(r, (r + i) % 4).start()

    for stage in range(3):
        each_peer(stage, lambda dy, dx: up1_of(at(dy, dx), g).wait_recv())

    @pl.loop(0, 2)
    def _(f):
        up1f_of(f, core).start()

    @pl.loop(0, 2)
    def _(f):
        up1f_of(f, 1 - core).wait_recv()

        @pl.loop(0, 8)
        def _(j):
            subtract(pparent, pfront, pupper1, f, f * 8 + j, 16)

    @pl.loop(0, 8)
    def _(j):
        extend(pfront, pparent, 2, j, j + 8)

    @pl.loop(1, 4)
    def _(i):
        piv2_of((r + i) % 4, r).wait_recv()

    upper[0] = jnp.dot(
        inv[6], piv2[...].reshape(PANEL, WIDTH).astype(BF16), preferred_element_type=F32
    ).astype(BF16)

    def out_of(slab, to):
        return remote(
            front.at[to], out.at[:, :, columns(slab)],
            out_send.at[to], out_recv.at[slab], to * 4 + r, panel,
        )

    def finish(dy, dx):
        to = at(dy, dx)
        subtract(parent, front, upper, 0, to, 8)
        out_of(g, to).start()

    for stage in (2, 1, 0):
        each_peer(stage, finish)
    subtract(parent, front, upper, 0, g, 8)
    out_copy = pltpu.make_async_copy(front.at[g], out.at[:, :, columns(g)], local_sem.at[0])
    out_copy.start()
    out_copy.wait()

    def settle(dy, dx):
        slab = at(dy, dx)
        out_of(slab, g).wait_recv()
        out_of(g, slab).wait_send()
        a2a_of(g, slab).wait_send()
        map_of(g, slab).wait_send()
        up0_of(g, slab).wait_send()
        up1_of(g, slab).wait_send()

    for stage in range(3):
        each_peer(stage, settle)

    @pl.loop(0, 4)
    def _(f):
        up0f_of(f, core).wait_send()

    @pl.loop(0, 2)
    def _(f):
        up1f_of(f, core).wait_send()

    @pl.loop(1, 4)
    def _(i):
        piv2_of(r, (r + i) % 4).wait_send()


def on_device(child_front, own_map, cross_map, pivot_inverse):
    rows, width = child_front.shape
    maps = jnp.concatenate([own_map[:, 0, :], cross_map[:, 0, :]], axis=1)
    maps = jnp.pad(maps, ((0, 8 - maps.shape[0]), (0, 128 - maps.shape[1])))
    dma = pltpu.SemaphoreType.DMA
    call = pl.pallas_call(
        kernel,
        out_shape=jax.ShapeDtypeStruct((2, BLOCK, width), BF16),
        in_specs=[
            pl.BlockSpec(memory_space=pl.ANY),
            pl.BlockSpec(memory_space=pltpu.VMEM),
            pl.BlockSpec(memory_space=pl.ANY),
        ],
        out_specs=pl.BlockSpec(memory_space=pl.ANY),
        scratch_shapes=[
            pltpu.VMEM((16, 2, BLOCK, WIDTH), BF16),
            pltpu.VMEM((16, 2, BLOCK, WIDTH), BF16),
            pltpu.VMEM((16, 2, BLOCK, PANEL), BF16),
            pltpu.VMEM((16, 2, BLOCK, PANEL), BF16),
            pltpu.VMEM((7, PANEL, PANEL), BF16),
            pltpu.VMEM((16, 8, 128), jnp.int32),
            pltpu.SMEM((16, 8, 128), jnp.int32),
            pltpu.VMEM((16, 4, 32, WIDTH), BF16),
            pltpu.VMEM((16, 4, 16, WIDTH), BF16),
            pltpu.VMEM((16, 4, 8, WIDTH), F32),
            pltpu.VMEM((4, 4, 32, BLOCK), BF16),
            pltpu.VMEM((8, 4, 16, BLOCK), BF16),
            pltpu.VMEM((4, PANEL, WIDTH), BF16),
            pltpu.VMEM((4, PANEL, PANEL), BF16),
            pltpu.VMEM((2, PANEL, PANEL), BF16),
            dma((16,)), dma((16,)), dma((16,)), dma((16,)), dma((3,)), dma((1,)),
            dma((16,)), dma((16,)), dma((4,)), dma((4,)), dma((4, 4)), dma((4, 4)),
            dma((4,)), dma((4,)), dma((4,)), dma((4,)), dma((4,)), dma((4,)),
            dma((4,)), dma((4,)), dma((16,)), dma((16,)), dma((4,)), dma((4,)),
            dma((16,)), dma((16,)), dma((2,)), dma((2,)), dma((16,)), dma((16,)), dma((4,)),
        ],
        compiler_params=pltpu.CompilerParams(
            collective_id=0, has_side_effects=True, vmem_limit_bytes=48 * 1024 * 1024
        ),
        cost_estimate=pl.CostEstimate(
            flops=9_000_000_000, bytes_accessed=16_000_000, transcendentals=0
        ),
    )
    result = call(child_front.reshape(2, BLOCK, width), maps, pivot_inverse)
    return result.reshape(rows, width)


def solution(mesh):
    placed = (P("leaf", "panel"), P(None, "leaf", None), P(None, "leaf", None), P())
    return jax.shard_map(
        on_device, mesh=mesh, in_specs=placed, out_specs=P("leaf", "panel"), check_vma=False
    )
```

time: 539 us -> 173 us (0.32)
  waiting for transfers between devices: 446 us -> 0 us
  Pallas kernels: 0 us -> 165 us
  matrix products: 42.6 us -> 0 us
  starting transfers between devices: 18.4 us -> 0 us
  between operations: 13.4 us -> 0.01 us
  other arithmetic: 12.3 us -> 0.08 us
    ppermute x18 -> x0, waiting for transfers between devices: 283 us -> none  [swapped(): return lax.ppermute(block, axis, route)]
    pallas_call x0 -> x1, Pallas kernels: none -> 165 us  [on_device(): result = call(child_front.reshape(2, BLOCK, width), maps, pivot_inverse)]
    psum x3 -> x0, waiting for transfers between devices: 163 us -> none  [spread(): return lax.psum(block, axis)]
    dot_general x9 -> x0, matrix products: 42.6 us -> none  [the longest x3 21.5 us: on_device(): jnp.dot(columns, upper_rows, preferred_element_type=jnp.float32)]
    ppermute x18 -> x0, starting transfers between devices: 18.3 us -> none  [swapped(): return lax.ppermute(block, axis, route)]
    select_n x15 -> x0, other arithmetic: 12.3 us -> none  [the longest x12 10.1 us: collect_pivots(): jnp.where(upper_half, jnp.concatenate([received, buffer], axis=0), jnp.co...]
  transfers between devices with their start and end apart: 21 -> 0, of which waited for: 18 -> 0; matrix products, arithmetic and copies ran while one was open for 3% -> 0% of each run, Pallas kernels for 0% -> 0%
where the time goes in v1:
time: 173 us; the launch traced here: 170 us
  Pallas kernels  165 us (95%)
  local copies, waits for them, and re-layouts  4.45 us (3%)
    pallas_call x1, Pallas kernels, on_device(): result = call(child_front.reshape(2, BLOCK, width), maps, pivot_inverse)  165 us

profile of v1, /device:TPU:1, one launch (start us, length us, event | category | flops | bytes accessed | tf_op | source)
XLA Modules:
  0.0 169.8 jit_solution(12458099371585338820)
XLA Ops:
  0.0 0.8 copy.5
  0.8 0.8 copy.6
  1.5 0.1 pad_add_fusion
  1.6 0.0 copy-start
  1.6 1.6 copy-done
  3.2 165.3 %shard_map.46 = bf16[2,128,4096]{2,1,0:T(8,128)(2,1)S(1)} custom-call(bf16[2,128,4096]{2,1,0:T(8,128)(2,1)S(1)} %bitcast.5, s32[8,128]{1,0:T(8,128)S(1)} %pad.4.maps, bf16[7,512,512]{2,1,0:T(8,128)(2,1)} %inverse.1), custom_call_target="tpu_custom_call" | custom-call | flops 8999999488 | bytes 16000000 | tf_op jit(solution)/shard_map/pallas_call | solution.py:525
  168.5 1.3 copy.8
  (1 shorter events, 0.0 us)
Async XLA Ops:
  1.6 1.6 copy-start

commit v2 on v1

--- a/solution.py
+++ b/solution.py
@@ -22,7 +22,7 @@
 def kernel(
     child, maps, inverse, out,
     front, parent, pfront, pparent, inv, map_buf, map_tab,
-    piv0, piv1, piv2, ppiv0, ppiv1, upper, pupper0, pupper1,
+    piv0, piv1, piv2, piv2_wide, ppiv0, ppiv1, upper, pupper0, pupper1,
     map_send, map_recv, a2a_send, a2a_recv, first_send, first_recv,
     pan_send, pan_recv, fwd_send, fwd_recv, piv0_send, piv0_recv,
     piv1_send, piv1_recv, piv2_send, piv2_recv, pp0_send, pp0_recv,
@@ -60,6 +60,55 @@
             device_id=(to_leaf, to_panel), device_id_type=MESH,
         )
 
+    def crossed(first, second):
+        return at(core * first + (1 - core) * second, core * second + (1 - core) * first)
+
+    class Spread:
+        def __init__(self, part_of, send, recv):
+            self.part_of, self.send, self.recv = part_of, send, recv
+
+        def copy(self, slab, i, j, to):
+            part = self.part_of(slab)
+            return remote(part, part, self.send.at[i, j], self.recv.at[slab], to * 4 + r, panel)
+
+        def begin(self):
+            @pl.loop(1, 4)
+            def _(i):
+                self.copy(g, i, 0, crossed(i, 0)).start()
+                self.copy(g, 0, i, crossed(0, i)).start()
+
+        def pass_on(self):
+            @pl.loop(1, 4)
+            def _(i):
+                slab = crossed(i, 0)
+                self.copy(slab, 0, 0, g).wait_recv()
+
+                @pl.loop(1, 4)
+                def _(j):
+                    self.copy(slab, i, j, crossed(0, j)).start()
+
+        def take_direct(self):
+            @pl.loop(1, 4)
+            def _(j):
+                self.copy(crossed(0, j), 0, 0, g).wait_recv()
+
+        def take_passed(self):
+            @pl.loop(1, 4)
+            def _(i):
+                @pl.loop(1, 4)
+                def _(j):
+                    self.copy(crossed(i, j), 0, 0, g).wait_recv()
+
+        def sent(self):
+            @pl.loop(1, 4)
+            def _(i):
+                self.copy(g, i, 0, crossed(i, 0)).wait_send()
+                self.copy(g, 0, i, crossed(0, i)).wait_send()
+
+                @pl.loop(1, 4)
+                def _(j):
+                    self.copy(crossed(i, 0), i, j, crossed(0, j)).wait_send()
+
     barrier = pltpu.get_barrier_semaphore()
 
     def greet(dy, dx):
@@ -105,17 +154,13 @@
     def a2a_of(slab, to):
         return remote(child.at[:, :, columns(to)], front.at[slab], a2a_send.at[to], a2a_recv.at[slab], to * 4 + r, panel)
 
-    def pan_of(slab, to):
-        return remote(pfront.at[slab, core], pfront.at[slab, core], pan_send.at[to], pan_recv.at[slab], to * 4 + r, panel)
+    spread_panel = Spread(lambda slab: pfront.at[slab, core], pan_send, pan_recv)
 
     def send_child(dy, dx):
         to = at(dy, dx)
         map_of(g, to).start()
         a2a_of(g, to).start()
 
-    def send_panel(dy, dx):
-        pan_of(g, at(dy, dx)).start()
-
     each_peer(0, send_child)
 
     @pl.when(panel == 0)
@@ -126,11 +171,9 @@
     def _():
         first_copy(core, panel, 0).wait_recv()
 
-    each_peer(0, send_panel)
+    spread_panel.begin()
     each_peer(1, send_child)
-    each_peer(1, send_panel)
     each_peer(2, send_child)
-    each_peer(2, send_panel)
 
     own_copy.wait()
     map_copy.wait()
@@ -180,8 +223,6 @@
         return remote(part, part, fwd_send.at[f], fwd_recv.at[f], leaf, mate)
 
     def open_front(f):
-        fwd_of(f, core).start()
-
         @pl.loop(0, 2)
         def _(j):
             extend(front, parent, 0, f * 4 + j, f * 4 + j + 2)
@@ -203,7 +244,6 @@
 
     def take_slab(dy, dx):
         a2a_of(at(dy, dx), g).wait_recv()
-        pan_of(at(dy, dx), g).wait_recv()
 
     piece = pl.ds(multiple(x * BLOCK, BLOCK), BLOCK)
 
@@ -213,11 +253,12 @@
             pp0_send.at[to], pp0_recv.at[owner], g * 4 + to, panel,
         )
 
-    def up0_of(slab, to):
-        part = pupper0.at[
+    spread_upper0 = Spread(
+        lambda slab: pupper0.at[
             slab // 4, pl.ds(multiple(core * 256, 256), 256), pl.ds(multiple(slab % 4 * BLOCK, BLOCK), BLOCK)
-        ]
-        return remote(part, part, up0_send.at[to], up0_recv.at[slab], to * 4 + r, panel)
+        ],
+        up0_send, up0_recv,
+    )
 
     def up0f_of(f, half):
         part = pupper0.at[f, pl.ds(multiple(half * 256, 256), 256), :]
@@ -225,6 +266,9 @@
 
     each_peer(0, take_slab)
     open_front(y)
+    spread_panel.pass_on()
+    spread_panel.take_direct()
+    fwd_of(y, core).start()
     open_panel(y)
 
     @pl.loop(1, 4)
@@ -235,6 +279,9 @@
     def _(j):
         ppiv0[j, r] = pparent[y * 4 + j, 0, 0:32, piece]
 
+    each_peer(1, take_slab)
+    open_front((y + 1) % 4)
+    open_front((y + 3) % 4)
     inv_copy.wait()
 
     @pl.loop(1, 4)
@@ -245,38 +292,105 @@
     pupper0[y, half0, piece] = jnp.dot(
         inv[y, half0, :], ppiv0[...].reshape(PANEL, BLOCK), preferred_element_type=F32
     ).astype(BF16)
-    for stage in range(3):
-        each_peer(stage, lambda dy, dx: up0_of(g, at(dy, dx)).start())
-
-    each_peer(1, take_slab)
-    open_front((y + 1) % 4)
-    open_front((y + 3) % 4)
-    open_panel((y + 1) % 4)
-    open_panel((y + 3) % 4)
+    spread_upper0.begin()
+
     each_peer(2, take_slab)
     open_front((y + 2) % 4)
-    open_panel((y + 2) % 4)
-
-    each_peer(0, lambda dy, dx: up0_of(at(dy, dx), g).wait_recv())
-    up0f_of(y, core).start()
-    each_peer(1, lambda dy, dx: up0_of(at(dy, dx), g).wait_recv())
-    up0f_of((y + 1) % 4, core).start()
-    up0f_of((y + 3) % 4, core).start()
-    each_peer(2, lambda dy, dx: up0_of(at(dy, dx), g).wait_recv())
-    up0f_of((y + 2) % 4, core).start()
+    spread_panel.take_passed()
+
+    @pl.loop(1, 4)
+    def _(i):
+        fwd_of((y + i) % 4, core).start()
+
+    @pl.loop(1, 4)
+    def _(i):
+        open_panel((y + i) % 4)
+
+    spread_upper0.pass_on()
+
+    @pl.loop(0, 4)
+    def _(i):
+        f = (y + i + i // 2 - 2 * (i // 3)) % 4
+
+        @pl.loop(1, 4)
+        def _(i):
+            piv0_of(f, (r + i) % 4, r).wait_recv()
+
+        upper[f] = jnp.dot(
+            inv[f], piv0[pl.ds(f * 4, 4)].reshape(PANEL, WIDTH), preferred_element_type=F32
+        ).astype(BF16)
+
+        @pl.loop(0, 4)
+        def _(j):
+            subtract(parent, front, upper, f, f * 4 + j, 32)
+
+    @pl.loop(0, 4)
+    def _(f):
+        @pl.loop(1, 4)
+        def _(i):
+            piv0_of(f, r, (r + i) % 4).wait_send()
+
+    def piv1_of(owner, to):
+        return remote(
+            parent.at[:, 0, pl.ds(0, 16), :], piv1.at[:, owner],
+            piv1_send.at[to], piv1_recv.at[owner], g * 4 + to, panel,
+        )
+
+    def pp1_of(owner, to):
+        return remote(
+            pparent.at[pl.ds(y // 2 * 8, 8), 0, pl.ds(0, 16), piece], ppiv1.at[:, owner],
+            pp1_send.at[to], pp1_recv.at[owner], g * 4 + to, panel,
+        )
+
+    spread_upper1 = Spread(
+        lambda slab: pupper1.at[
+            slab // 8,
+            pl.ds(multiple(core * 256 + slab // 4 % 2 * BLOCK, BLOCK), BLOCK),
+            pl.ds(multiple(slab % 4 * BLOCK, BLOCK), BLOCK),
+        ],
+        up1_send, up1_recv,
+    )
+
+    def up1f_of(f, half):
+        part = pupper1.at[f, pl.ds(multiple(half * 256, 256), 256), :]
+        return remote(part, part, up1f_send.at[f], up1f_recv.at[f], leaf, mate)
+
+    @pl.loop(0, 2)
+    def _(f):
+        @pl.loop(0, 4)
+        def _(j):
+            extend(front, parent, 1, f * 8 + j, f * 8 + j + 4)
+
+    @pl.loop(1, 4)
+    def _(i):
+        piv1_of(r, (r + i) % 4).start()
+
+    @pl.loop(0, 16)
+    def _(j):
+        piv1[j, r] = parent[j, 0, 0:16, :]
+
+    spread_upper0.take_direct()
+    spread_upper0.take_passed()
+
+    @pl.loop(0, 4)
+    def _(f):
+        up0f_of(f, core).start()
 
     @pl.when(panel == 0)
     def _():
         for index in range(3):
             first_copy(0, 1, index).wait_send()
 
-    for stage in range(3):
-        each_peer(stage, lambda dy, dx: pan_of(g, at(dy, dx)).wait_send())
+    spread_panel.sent()
 
     @pl.loop(0, 4)
     def _(f):
         fwd_of(f, core).wait_send()
 
+    @pl.loop(1, 4)
+    def _(i):
+        pp0_of(r, (r + i) % 4).wait_send()
+
     @pl.loop(0, 4)
     def _(f):
         up0f_of(f, 1 - core).wait_recv()
@@ -284,68 +398,6 @@
         @pl.loop(0, 4)
         def _(j):
             subtract(pparent, pfront, pupper0, f, f * 4 + j, 32)
-
-    @pl.loop(0, 4)
-    def _(f):
-        @pl.loop(1, 4)
-        def _(i):
-            piv0_of(f, (r + i) % 4, r).wait_recv()
-
-        upper[f] = jnp.dot(
-            inv[f], piv0[pl.ds(f * 4, 4)].reshape(PANEL, WIDTH), preferred_element_type=F32
-        ).astype(BF16)
-
-        @pl.loop(0, 4)
-        def _(j):
-            subtract(parent, front, upper, f, f * 4 + j, 32)
-
-    @pl.loop(0, 4)
-    def _(f):
-        @pl.loop(1, 4)
-        def _(i):
-            piv0_of(f, r, (r + i) % 4).wait_send()
-
-    @pl.loop(1, 4)
-    def _(i):
-        pp0_of(r, (r + i) % 4).wait_send()
-
-    def piv1_of(owner, to):
-        return remote(
-            parent.at[:, 0, pl.ds(0, 16), :], piv1.at[:, owner],
-            piv1_send.at[to], piv1_recv.at[owner], g * 4 + to, panel,
-        )
-
-    def pp1_of(owner, to):
-        return remote(
-            pparent.at[pl.ds(y // 2 * 8, 8), 0, pl.ds(0, 16), piece], ppiv1.at[:, owner],
-            pp1_send.at[to], pp1_recv.at[owner], g * 4 + to, panel,
-        )
-
-    def up1_of(slab, to):
-        part = pupper1.at[
-            slab // 8,
-            pl.ds(multiple(core * 256 + slab // 4 % 2 * BLOCK, BLOCK), BLOCK),
-            pl.ds(multiple(slab % 4 * BLOCK, BLOCK), BLOCK),
-        ]
-        return remote(part, part, up1_send.at[to], up1_recv.at[slab], to * 4 + r, panel)
-
-    def up1f_of(f, half):
-        part = pupper1.at[f, pl.ds(multiple(half * 256, 256), 256), :]
-        return remote(part, part, up1f_send.at[f], up1f_recv.at[f], leaf, mate)
-
-    @pl.loop(0, 2)
-    def _(f):
-        @pl.loop(0, 4)
-        def _(j):
-            extend(front, parent, 1, f * 8 + j, f * 8 + j + 4)
-
-    @pl.loop(1, 4)
-    def _(i):
-        piv1_of(r, (r + i) % 4).start()
-
-    @pl.loop(0, 16)
-    def _(j):
-        piv1[j, r] = parent[j, 0, 0:16, :]
 
     @pl.loop(0, 2)
     def _(f):
@@ -360,6 +412,16 @@
     @pl.loop(0, 8)
     def _(j):
         ppiv1[j, r] = pparent[y // 2 * 8 + j, 0, 0:16, piece]
+
+    @pl.loop(1, 4)
+    def _(i):
+        piv1_of((r + i) % 4, r).wait_recv()
+
+    @pl.loop(0, 2)
+    def _(f):
+        upper[f] = jnp.dot(
+            inv[4 + f], piv1[pl.ds(f * 8, 8)].reshape(PANEL, WIDTH), preferred_element_type=F32
+        ).astype(BF16)
 
     @pl.loop(1, 4)
     def _(i):
@@ -369,19 +431,10 @@
     pupper1[y // 2, quarter, piece] = jnp.dot(
         inv[4 + y // 2, quarter, :], ppiv1[...].reshape(PANEL, BLOCK), preferred_element_type=F32
     ).astype(BF16)
-    for stage in range(3):
-        each_peer(stage, lambda dy, dx: up1_of(g, at(dy, dx)).start())
-
-    @pl.loop(1, 4)
-    def _(i):
-        piv1_of((r + i) % 4, r).wait_recv()
-
-    @pl.loop(0, 2)
-    def _(f):
-        upper[f] = jnp.dot(
-            inv[4 + f], piv1[pl.ds(f * 8, 8)].reshape(PANEL, WIDTH), preferred_element_type=F32
-        ).astype(BF16)
-
+    spread_upper1.begin()
+
+    @pl.loop(0, 2)
+    def _(f):
         @pl.loop(0, 8)
         def _(j):
             subtract(parent, front, upper, f, f * 8 + j, 16)
@@ -393,24 +446,25 @@
 
     def piv2_of(owner, to):
         return remote(
-            piv2.at[:, owner], piv2.at[:, owner],
-            piv2_send.at[to], piv2_recv.at[owner], g * 4 + to, panel,
+            piv2.at[owner], piv2.at[owner], piv2_send.at[to], piv2_recv.at[owner], g * 4 + to, panel,
         )
 
     @pl.loop(0, 8)
     def _(j):
         extend(front, parent, 2, j, j + 8)
 
-    @pl.loop(0, 16)
+    @pl.loop(0, 8)
     def _(j):
-        piv2[j, r] = parent[j, 0, 0:16, :].astype(F32)[0:8]
+        pair = [parent[2 * j + k, 0, 0:16, :].astype(F32)[0:8] for k in range(2)]
+        piv2[r, j] = jnp.concatenate(pair, axis=0).astype(BF16)
 
     @pl.loop(1, 4)
     def _(i):
         piv2_of(r, (r + i) % 4).start()
 
-    for stage in range(3):
-        each_peer(stage, lambda dy, dx: up1_of(at(dy, dx), g).wait_recv())
+    spread_upper1.pass_on()
+    spread_upper1.take_direct()
+    spread_upper1.take_passed()
 
     @pl.loop(0, 2)
     def _(f):
@@ -432,8 +486,16 @@
     def _(i):
         piv2_of((r + i) % 4, r).wait_recv()
 
+    @pl.loop(0, 4)
+    def _(owner):
+        @pl.loop(0, 8)
+        def _(j):
+            both = piv2[owner, j].astype(F32)
+            piv2_wide[2 * j, owner] = both[0:8]
+            piv2_wide[2 * j + 1, owner] = both[8:16]
+
     upper[0] = jnp.dot(
-        inv[6], piv2[...].reshape(PANEL, WIDTH).astype(BF16), preferred_element_type=F32
+        inv[6], piv2_wide[...].reshape(PANEL, WIDTH).astype(BF16), preferred_element_type=F32
     ).astype(BF16)
 
     def out_of(slab, to):
@@ -460,11 +522,12 @@
         out_of(g, slab).wait_send()
         a2a_of(g, slab).wait_send()
         map_of(g, slab).wait_send()
-        up0_of(g, slab).wait_send()
-        up1_of(g, slab).wait_send()
 
     for stage in range(3):
         each_peer(stage, settle)
+
+    spread_upper0.sent()
+    spread_upper1.sent()
 
     @pl.loop(0, 4)
     def _(f):
@@ -503,6 +566,7 @@
             pltpu.SMEM((16, 8, 128), jnp.int32),
             pltpu.VMEM((16, 4, 32, WIDTH), BF16),
             pltpu.VMEM((16, 4, 16, WIDTH), BF16),
+            pltpu.VMEM((4, 8, 16, WIDTH), BF16),
             pltpu.VMEM((16, 4, 8, WIDTH), F32),
             pltpu.VMEM((4, 4, 32, BLOCK), BF16),
             pltpu.VMEM((8, 4, 16, BLOCK), BF16),
@@ -510,13 +574,13 @@
             pltpu.VMEM((4, PANEL, PANEL), BF16),
             pltpu.VMEM((2, PANEL, PANEL), BF16),
             dma((16,)), dma((16,)), dma((16,)), dma((16,)), dma((3,)), dma((1,)),
-            dma((16,)), dma((16,)), dma((4,)), dma((4,)), dma((4, 4)), dma((4, 4)),
+            dma((4, 4)), dma((16,)), dma((4,)), dma((4,)), dma((4, 4)), dma((4, 4)),
             dma((4,)), dma((4,)), dma((4,)), dma((4,)), dma((4,)), dma((4,)),
-            dma((4,)), dma((4,)), dma((16,)), dma((16,)), dma((4,)), dma((4,)),
-            dma((16,)), dma((16,)), dma((2,)), dma((2,)), dma((16,)), dma((16,)), dma((4,)),
+            dma((4,)), dma((4,)), dma((4, 4)), dma((16,)), dma((4,)), dma((4,)),
+            dma((4, 4)), dma((16,)), dma((2,)), dma((2,)), dma((16,)), dma((16,)), dma((4,)),
         ],
         compiler_params=pltpu.CompilerParams(
-            collective_id=0, has_side_effects=True, vmem_limit_bytes=48 * 1024 * 1024
+            collective_id=0, has_side_effects=True, vmem_limit_bytes=60 * 1024 * 1024
         ),
         cost_estimate=pl.CostEstimate(
             flops=9_000_000_000, bytes_accessed=16_000_000, transcendentals=0

time: 173 us -> 151 us (0.87); the launches traced: 170 us -> 150 us
  Pallas kernels: 165 us -> 145 us
    pallas_call x1, Pallas kernels: 165 us -> 145 us  [on_device(): result = call(child_front.reshape(2, BLOCK, width), maps, pivot_inverse)]
where the time goes in v2:
time: 151 us; the launch traced here: 150 us
  Pallas kernels  145 us (96%)
  local copies, waits for them, and re-layouts  5.26 us (3%)
    pallas_call x1, Pallas kernels, on_device(): result = call(child_front.reshape(2, BLOCK, width), maps, pivot_inverse)  145 us
    unnamed x1, local copies, waits for them, and re-layouts  3.13 us

profile of v2, /device:TPU:1, one launch (start us, length us, event | category | flops | bytes accessed | tf_op | source)
XLA Modules:
  0.0 150.1 jit_solution(9506654280102143186)
XLA Ops:
  0.0 0.8 copy.5
  0.8 0.8 copy.6
  1.5 0.1 pad_add_fusion
  1.6 0.6 pad.4.maps
  2.2 144.7 %shard_map.46 = bf16[2,128,4096]{2,1,0:T(8,128)(2,1)} custom-call(bf16[2,128,4096]{2,1,0:T(8,128)(2,1)} %bitcast.7, s32[8,128]{1,0:T(8,128)} %pad.4.maps, bf16[7,512,512]{2,1,0:T(8,128)(2,1)} %inverse.1), custom_call_target="tpu_custom_call" | custom-call | flops 8999999488 | bytes 16000000 | tf_op jit(solution)/shard_map/pallas_call | solution.py:589
  146.9 3.1 %copy.8 = bf16[256,4096]{1,0:T(8,128)(2,1)} copy(bf16[256,4096]{1,0:T(8,128)(2,1)} %bitcast.4) | data formatting | bytes 4194304

commit v3 on v2

v3 whole, which is shorter than its diff:
```python
import functools

import jax
import jax.numpy as jnp
from jax import lax
from jax.experimental import pallas as pl
from jax.experimental.pallas import tpu as pltpu
from jax.sharding import PartitionSpec as P

PANEL = 512
BLOCK = 128
WIDTH = 256
HALF = 128
MESH = pl.DeviceIdType.MESH
F32 = jnp.float32
BF16 = jnp.bfloat16


def multiple(value, of):
    return pl.multiple_of(value, of)


def kernel(
    child, maps, inverse, out,
    front, parent, pfront, pparent0, pparent1, pparent2, inv, map_buf, map_tab,
    piv0, piv1, piv2, piv2_wide, ppiv0, ppiv1, upper, pupper0, pupper1,
    map_send, map_recv, a2a_send, a2a_recv, first_send, first_recv,
    pan_send, pan_recv, fwd_send, fwd_recv, piv0_send, piv0_recv,
    piv1_send, piv1_recv, piv2_send, piv2_recv, pp0_send, pp0_recv,
    pp1_send, pp1_recv, up0_send, up0_recv, up0f_send, up0f_recv,
    up1_send, up1_recv, up1f_send, up1f_recv, out_send, out_recv, local_sem,
):
    leaf = lax.axis_index("leaf")
    panel = lax.axis_index("panel")
    g, r = leaf // 4, leaf % 4
    y, x = g // 4, g % 4
    core = panel % 2
    mate = panel + 1 - 2 * core

    def at(dy, dx):
        return ((y + dy) % 4) * 4 + (x + dx) % 4

    def each_peer(stage, visit):
        if stage == 0:
            @pl.loop(1, 4)
            def _(i):
                visit(0, i)
        elif stage == 1:
            @pl.loop(0, 4)
            def _(i):
                visit(1, i)
                visit(3, i)
        else:
            @pl.loop(0, 4)
            def _(i):
                visit(2, i)

    def remote(src, dst, send, recv, to_leaf, to_panel):
        return pltpu.make_async_remote_copy(
            src_ref=src, dst_ref=dst, send_sem=send, recv_sem=recv,
            device_id=(to_leaf, to_panel), device_id_type=MESH,
        )

    def crossed(first, second):
        return at(core * first + (1 - core) * second, core * second + (1 - core) * first)

    class Spread:
        def __init__(self, part_of, send, recv):
            self.part_of, self.send, self.recv = part_of, send, recv

        def copy(self, slab, i, j, to):
            part = self.part_of(slab)
            return remote(part, part, self.send.at[i, j], self.recv.at[slab], to * 4 + r, panel)

        def begin(self):
            @pl.loop(1, 4)
            def _(i):
                self.copy(g, i, 0, crossed(i, 0)).start()
                self.copy(g, 0, i, crossed(0, i)).start()

        def pass_on(self):
            @pl.loop(1, 4)
            def _(i):
                slab = crossed(i, 0)
                self.copy(slab, 0, 0, g).wait_recv()

                @pl.loop(1, 4)
                def _(j):
                    self.copy(slab, i, j, crossed(0, j)).start()

        def take_direct(self):
            @pl.loop(1, 4)
            def _(j):
                self.copy(crossed(0, j), 0, 0, g).wait_recv()

        def take_passed(self):
            @pl.loop(1, 4)
            def _(i):
                @pl.loop(1, 4)
                def _(j):
                    self.copy(crossed(i, j), 0, 0, g).wait_recv()

        def sent(self):
            @pl.loop(1, 4)
            def _(i):
                self.copy(g, i, 0, crossed(i, 0)).wait_send()
                self.copy(g, 0, i, crossed(0, i)).wait_send()

                @pl.loop(1, 4)
                def _(j):
                    self.copy(crossed(i, 0), i, j, crossed(0, j)).wait_send()

    barrier = pltpu.get_barrier_semaphore()

    def greet(dy, dx):
        pl.semaphore_signal(barrier, inc=1, device_id=(at(dy, dx) * 4 + r, panel), device_id_type=MESH)

    for stage in range(3):
        each_peer(stage, greet)

    @pl.loop(1, 4)
    def _(i):
        pl.semaphore_signal(barrier, inc=1, device_id=(g * 4 + (r + i) % 4, panel), device_id_type=MESH)
        pl.semaphore_signal(barrier, inc=1, device_id=(leaf, (panel + i) % 4), device_id_type=MESH)

    def columns(which, h):
        return pl.ds(multiple(which * WIDTH + h * HALF, HALF), HALF)

    def own_copy(h):
        return pltpu.make_async_copy(child.at[:, :, columns(g, h)], front.at[h, g], local_sem.at[4 + h])

    own_copy(0).start()
    own_copy(1).start()
    inv_copy = pltpu.make_async_copy(inverse, inv, local_sem.at[1])
    inv_copy.start()
    map_copy = pltpu.make_async_copy(maps, map_buf.at[g], local_sem.at[2])
    map_copy.start()
    pl.semaphore_wait(barrier, 21)

    def first_copy(half, to_panel, index):
        return remote(
            child.at[half, :, pl.ds(0, PANEL)], pfront.at[g, half],
            first_send.at[index], first_recv.at[0], leaf, to_panel,
        )

    first_own = pltpu.make_async_copy(child.at[0, :, pl.ds(0, PANEL)], pfront.at[g, 0], local_sem.at[3])

    @pl.when(panel == 0)
    def _():
        first_copy(0, 2, 1).start()
        first_copy(1, 3, 2).start()
        first_copy(1, 1, 0).start()
        first_own.start()

    def map_of(slab, to):
        return remote(maps, map_buf.at[slab], map_send.at[to], map_recv.at[slab], to * 4 + r, panel)

    def a2a_of(h, slab, to):
        return remote(
            child.at[:, :, columns(to, h)], front.at[h, slab],
            a2a_send.at[h, to], a2a_recv.at[h, slab], to * 4 + r, panel,
        )

    spread_panel = Spread(lambda slab: pfront.at[slab, core], pan_send, pan_recv)

    def send_child(h, stage):
        each_peer(stage, lambda dy, dx: a2a_of(h, g, at(dy, dx)).start())

    for stage in range(3):
        each_peer(stage, lambda dy, dx: map_of(g, at(dy, dx)).start())
    for stage in range(3):
        send_child(0, stage)

    @pl.when(panel == 0)
    def _():
        first_own.wait()

    @pl.when(panel != 0)
    def _():
        first_copy(core, panel, 0).wait_recv()

    spread_panel.begin()

    map_copy.wait()

    def take_map(dy, dx):
        map_of(at(dy, dx), g).wait_recv()

    for stage in range(3):
        each_peer(stage, take_map)
    to_smem = pltpu.make_async_copy(map_buf, map_tab, local_sem.at[2])
    to_smem.start()
    to_smem.wait()

    def extend(src, dst, level, a, b):
        width = src.shape[3]
        step = min(width, WIDTH)
        for mine, other in ((a, b), (b, a)):
            for slot in range(2):
                from_own = map_tab[mine, level, slot] == 0
                from_cross = map_tab[mine, level, 2 + slot] == 0

                @pl.loop(0, BLOCK // 32)
                def _(q):
                    for left in range(0, width, step):
                        part = (pl.ds(multiple(q * 32, 32), 32), pl.ds(left, step))
                        kept = jnp.where(from_own, src[(mine, 0) + part], src[(mine, 1) + part])
                        moved = jnp.where(from_cross, src[(other, 0) + part], src[(other, 1) + part])
                        dst[(mine, slot) + part] = (kept.astype(F32) + moved.astype(F32)).astype(BF16)

    def subtract(src, columns_of, dst, factor, slab, rows):
        width = src.shape[3]
        step = min(width, WIDTH)
        left = columns_of[slab].reshape(2 * BLOCK, PANEL)
        keep = lax.broadcasted_iota(jnp.int32, (2 * BLOCK, step), 0) >= rows
        for low in range(0, width, step):
            part = pl.ds(low, step)
            product = jnp.dot(left, factor[:, part], preferred_element_type=F32)
            start = src[slab, :, :, part].reshape(2 * BLOCK, step).astype(F32)
            reduced = jnp.where(keep, start - product, 0.0).astype(BF16)
            dst[slab, :, :, part] = reduced.reshape(2, BLOCK, step)

    def piv0_of(h, f, owner, to):
        slabs = pl.ds(f * 4, 4)
        return remote(
            parent.at[h, slabs, 0, pl.ds(0, 32), :], piv0.at[h, slabs, owner],
            piv0_send.at[h, f, to], piv0_recv.at[h, f, owner], g * 4 + to, panel,
        )

    def fwd_of(f, half):
        part = pfront.at[pl.ds(f * 4, 4), half]
        return remote(part, part, fwd_send.at[f], fwd_recv.at[f], leaf, mate)

    def open_front(h, f):
        @pl.loop(0, 2)
        def _(j):
            extend(front.at[h], parent.at[h], 0, f * 4 + j, f * 4 + j + 2)

        @pl.loop(1, 4)
        def _(i):
            piv0_of(h, f, r, (r + i) % 4).start()

        @pl.loop(0, 4)
        def _(j):
            piv0[h, f * 4 + j, r] = parent[h, f * 4 + j, 0, 0:32, :]

    def open_stage(h, stage):
        each_peer(stage, lambda dy, dx: a2a_of(h, at(dy, dx), g).wait_recv())
        if stage == 0:
            own_copy(h).wait()
            open_front(h, y)
        elif stage == 1:
            @pl.loop(0, 2)
            def _(i):
                open_front(h, (y + 1 + 2 * i) % 4)
        else:
            open_front(h, (y + 2) % 4)

    def open_panel(f):
        fwd_of(f, 1 - core).wait_recv()

        @pl.loop(0, 2)
        def _(j):
            extend(pfront, pparent0, 0, f * 4 + j, f * 4 + j + 2)

    piece = pl.ds(multiple(x * BLOCK, BLOCK), BLOCK)

    def pp0_of(owner, to):
        return remote(
            pparent0.at[pl.ds(y * 4, 4), 0, pl.ds(0, 32), piece], ppiv0.at[:, owner],
            pp0_send.at[to], pp0_recv.at[owner], g * 4 + to, panel,
        )

    spread_upper0 = Spread(
        lambda slab: pupper0.at[
            slab // 4, pl.ds(multiple(core * 256, 256), 256), pl.ds(multiple(slab % 4 * BLOCK, BLOCK), BLOCK)
        ],
        up0_send, up0_recv,
    )

    def up0f_of(f, half):
        part = pupper0.at[f, pl.ds(multiple(half * 256, 256), 256), :]
        return remote(part, part, up0f_send.at[f], up0f_recv.at[f], leaf, mate)

    def piv1_of(h, owner, to):
        return remote(
            parent.at[h, :, 0, pl.ds(0, 16), :], piv1.at[h, :, owner],
            piv1_send.at[h, to], piv1_recv.at[h, owner], g * 4 + to, panel,
        )

    def pp1_of(owner, to):
        return remote(
            pparent1.at[pl.ds(y // 2 * 8, 8), 0, pl.ds(0, 16), piece], ppiv1.at[:, owner],
            pp1_send.at[to], pp1_recv.at[owner], g * 4 + to, panel,
        )

    spread_upper1 = Spread(
        lambda slab: pupper1.at[
            slab // 8,
            pl.ds(multiple(core * 256 + slab // 4 % 2 * BLOCK, BLOCK), BLOCK),
            pl.ds(multiple(slab % 4 * BLOCK, BLOCK), BLOCK),
        ],
        up1_send, up1_recv,
    )

    def up1f_of(f, half):
        part = pupper1.at[f, pl.ds(multiple(half * 256, 256), 256), :]
        return remote(part, part, up1f_send.at[f], up1f_recv.at[f], leaf, mate)

    def piv2_of(h, owner, to):
        part = piv2.at[h, owner]
        return remote(part, part, piv2_send.at[h, to], piv2_recv.at[h, owner], g * 4 + to, panel)

    def out_of(h, slab, to):
        return remote(
            front.at[h, to], out.at[:, :, columns(slab, h)],
            out_send.at[h, to], out_recv.at[h, slab], to * 4 + r, panel,
        )

    def others(visit):
        @pl.loop(1, 4)
        def _(i):
            visit((r + i) % 4)

    def own_level0(h):
        @pl.loop(0, 4)
        def _(i):
            f = (y + i + i // 2 - 2 * (i // 3)) % 4
            others(lambda owner: piv0_of(h, f, owner, r).wait_recv())
            upper[h, f] = jnp.dot(
                inv[f], piv0[h, pl.ds(f * 4, 4)].reshape(PANEL, HALF), preferred_element_type=F32
            ).astype(BF16)

            @pl.loop(0, 4)
            def _(j):
                subtract(parent.at[h], pparent0, front.at[h], upper.at[h, f], f * 4 + j, 32)

        @pl.loop(0, 4)
        def _(f):
            others(lambda to: piv0_of(h, f, r, to).wait_send())

        @pl.loop(0, 8)
        def _(j):
            a = j + j // 4 * 4
            extend(front.at[h], parent.at[h], 1, a, a + 4)

        others(lambda to: piv1_of(h, r, to).start())

        @pl.loop(0, 16)
        def _(j):
            piv1[h, j, r] = parent[h, j, 0, 0:16, :]

    def own_level1(h):
        others(lambda owner: piv1_of(h, owner, r).wait_recv())

        @pl.loop(0, 2)
        def _(f):
            upper[h, f] = jnp.dot(
                inv[4 + f], piv1[h, pl.ds(f * 8, 8)].reshape(PANEL, HALF), preferred_element_type=F32
            ).astype(BF16)

            @pl.loop(0, 8)
            def _(j):
                subtract(parent.at[h], pparent1, front.at[h], upper.at[h, f], f * 8 + j, 16)

        others(lambda to: piv1_of(h, r, to).wait_send())

        @pl.loop(0, 8)
        def _(j):
            extend(front.at[h], parent.at[h], 2, j, j + 8)

        @pl.loop(0, 8)
        def _(j):
            pair = [parent[h, 2 * j + k, 0, 0:16, :].astype(F32)[0:8] for k in range(2)]
            piv2[h, r, j] = jnp.concatenate(pair, axis=0).astype(BF16)

        others(lambda to: piv2_of(h, r, to).start())

    def own_level2(h):
        others(lambda owner: piv2_of(h, owner, r).wait_recv())

        @pl.loop(0, 4)
        def _(owner):
            @pl.loop(0, 8)
            def _(j):
                both = piv2[h, owner, j].astype(F32)
                piv2_wide[2 * j, owner] = both[0:8]
                piv2_wide[2 * j + 1, owner] = both[8:16]

        upper[h, 0] = jnp.dot(
            inv[6], piv2_wide[...].reshape(PANEL, HALF).astype(BF16), preferred_element_type=F32
        ).astype(BF16)

        def finish(dy, dx):
            to = at(dy, dx)
            subtract(parent.at[h], pparent2, front.at[h], upper.at[h, 0], to, 8)
            out_of(h, g, to).start()

        for stage in range(3):
            each_peer(stage, finish)
        subtract(parent.at[h], pparent2, front.at[h], upper.at[h, 0], g, 8)
        home(h).start()

    def home(h):
        return pltpu.make_async_copy(front.at[h, g], out.at[:, :, columns(g, h)], local_sem.at[4 + h])

    for stage in range(3):
        open_stage(0, stage)
    spread_panel.pass_on()
    send_child(1, 0)
    spread_panel.take_direct()
    fwd_of(y, core).start()
    open_panel(y)
    others(lambda to: pp0_of(r, to).start())

    @pl.loop(0, 4)
    def _(j):
        ppiv0[j, r] = pparent0[y * 4 + j, 0, 0:32, piece]

    inv_copy.wait()
    others(lambda owner: pp0_of(owner, r).wait_recv())
    half0 = pl.ds(multiple(core * 256, 256), 256)
    pupper0[y, half0, piece] = jnp.dot(
        inv[y, half0, :], ppiv0[...].reshape(PANEL, BLOCK), preferred_element_type=F32
    ).astype(BF16)
    spread_upper0.begin()
    send_child(1, 1)
    send_child(1, 2)

    spread_panel.take_passed()

    @pl.loop(1, 4)
    def _(i):
        fwd_of((y + i) % 4, core).start()

    @pl.loop(1, 4)
    def _(i):
        open_panel((y + i) % 4)

    own_level0(0)
    spread_upper0.pass_on()
    open_stage(1, 0)

    spread_upper0.take_direct()
    spread_upper0.take_passed()

    @pl.loop(0, 4)
    def _(f):
        up0f_of(f, core).start()

    @pl.when(panel == 0)
    def _():
        for index in range(3):
            first_copy(0, 1, index).wait_send()

    spread_panel.sent()

    @pl.loop(0, 4)
    def _(f):
        fwd_of(f, core).wait_send()

    @pl.loop(0, 4)
    def _(f):
        up0f_of(f, 1 - core).wait_recv()

        @pl.loop(0, 4)
        def _(j):
            subtract(pparent0, pparent0, pfront, pupper0.at[f], f * 4 + j, 32)

    @pl.loop(0, 8)
    def _(j):
        a = j + j // 4 * 4
        extend(pfront, pparent1, 1, a, a + 4)

    others(lambda to: pp1_of(r, to).start())

    @pl.loop(0, 8)
    def _(j):
        ppiv1[j, r] = pparent1[y // 2 * 8 + j, 0, 0:16, piece]

    open_stage(1, 1)
    open_stage(1, 2)
    own_level1(0)

    others(lambda owner: pp1_of(owner, r).wait_recv())
    quarter = pl.ds(multiple(core * 256 + y % 2 * BLOCK, BLOCK), BLOCK)
    pupper1[y // 2, quarter, piece] = jnp.dot(
        inv[4 + y // 2, quarter, :], ppiv1[...].reshape(PANEL, BLOCK), preferred_element_type=F32
    ).astype(BF16)
    spread_upper1.begin()
    own_level0(1)
    spread_upper1.pass_on()
    spread_upper1.take_direct()
    spread_upper1.take_passed()

    @pl.loop(0, 2)
    def _(f):
        up1f_of(f, core).start()

    @pl.loop(0, 2)
    def _(f):
        up1f_of(f, 1 - core).wait_recv()

        @pl.loop(0, 8)
        def _(j):
            subtract(pparent1, pparent1, pfront, pupper1.at[f], f * 8 + j, 16)

    @pl.loop(0, 8)
    def _(j):
        extend(pfront, pparent2, 2, j, j + 8)

    own_level2(0)
    own_level1(1)
    own_level2(1)

    for h in range(2):
        home(h).wait()

    def settle(dy, dx):
        slab = at(dy, dx)
        map_of(g, slab).wait_send()
        for h in range(2):
            out_of(h, slab, g).wait_recv()
            out_of(h, g, slab).wait_send()
            a2a_of(h, g, slab).wait_send()

    for stage in range(3):
        each_peer(stage, settle)
    spread_upper0.sent()
    spread_upper1.sent()

    @pl.loop(0, 4)
    def _(f):
        up0f_of(f, core).wait_send()

    @pl.loop(0, 2)
    def _(f):
        up1f_of(f, core).wait_send()

    def leave(to):
        pp0_of(r, to).wait_send()
        pp1_of(r, to).wait_send()
        for h in range(2):
            piv2_of(h, r, to).wait_send()

    others(leave)


def on_device(child_front, own_map, cross_map, pivot_inverse):
    rows, width = child_front.shape
    maps = jnp.concatenate([own_map[:, 0, :], cross_map[:, 0, :]], axis=1)
    maps = jnp.pad(maps, ((0, 8 - maps.shape[0]), (0, 128 - maps.shape[1])))
    dma = pltpu.SemaphoreType.DMA
    call = pl.pallas_call(
        kernel,
        out_shape=jax.ShapeDtypeStruct((2, BLOCK, width), BF16),
        in_specs=[
            pl.BlockSpec(memory_space=pl.ANY),
            pl.BlockSpec(memory_space=pltpu.VMEM),
            pl.BlockSpec(memory_space=pl.ANY),
        ],
        out_specs=pl.BlockSpec(memory_space=pl.ANY),
        scratch_shapes=[
            pltpu.VMEM((2, 16, 2, BLOCK, HALF), BF16),
            pltpu.VMEM((2, 16, 2, BLOCK, HALF), BF16),
            pltpu.VMEM((16, 2, BLOCK, PANEL), BF16),
            pltpu.VMEM((16, 2, BLOCK, PANEL), BF16),
            pltpu.VMEM((16, 2, BLOCK, PANEL), BF16),
            pltpu.VMEM((16, 2, BLOCK, PANEL), BF16),
            pltpu.VMEM((7, PANEL, PANEL), BF16),
            pltpu.VMEM((16, 8, 128), jnp.int32),
            pltpu.SMEM((16, 8, 128), jnp.int32),
            pltpu.VMEM((2, 16, 4, 32, HALF), BF16),
            pltpu.VMEM((2, 16, 4, 16, HALF), BF16),
            pltpu.VMEM((2, 4, 8, 16, HALF), BF16),
            pltpu.VMEM((16, 4, 8, HALF), F32),
            pltpu.VMEM((4, 4, 32, BLOCK), BF16),
            pltpu.VMEM((8, 4, 16, BLOCK), BF16),
            pltpu.VMEM((2, 4, PANEL, HALF), BF16),
            pltpu.VMEM((4, PANEL, PANEL), BF16),
            pltpu.VMEM((2, PANEL, PANEL), BF16),
            dma((16,)), dma((16,)), dma((2, 16)), dma((2, 16)), dma((3,)), dma((1,)),
            dma((4, 4)), dma((16,)), dma((4,)), dma((4,)), dma((2, 4, 4)), dma((2, 4, 4)),
            dma((2, 4)), dma((2, 4)), dma((2, 4)), dma((2, 4)), dma((4,)), dma((4,)),
            dma((4,)), dma((4,)), dma((4, 4)), dma((16,)), dma((4,)), dma((4,)),
            dma((4, 4)), dma((16,)), dma((2,)), dma((2,)), dma((2, 16)), dma((2, 16)), dma((6,)),
        ],
        compiler_params=pltpu.CompilerParams(
            collective_id=0, has_side_effects=True, vmem_limit_bytes=60 * 1024 * 1024
        ),
        cost_estimate=pl.CostEstimate(
            flops=9_000_000_000, bytes_accessed=16_000_000, transcendentals=0
        ),
    )
    result = call(child_front.reshape(2, BLOCK, width), maps, pivot_inverse)
    return result.reshape(rows, width)


def solution(mesh):
    placed = (P("leaf", "panel"), P(None, "leaf", None), P(None, "leaf", None), P())
    return jax.shard_map(
        on_device, mesh=mesh, in_specs=placed, out_specs=P("leaf", "panel"), check_vma=False
    )
```

time: 151 us -> 142 us (0.940)
  Pallas kernels: 145 us -> 136 us
    pallas_call x1, Pallas kernels: 145 us -> 136 us  [on_device(): result = call(child_front.reshape(2, BLOCK, width), maps, pivot_inverse)]
where the time goes in v3:
time: 142 us
  Pallas kernels  136 us (96%)
  local copies, waits for them, and re-layouts  5.26 us (4%)
    pallas_call x1, Pallas kernels, on_device(): result = call(child_front.reshape(2, BLOCK, width), maps, pivot_inverse)  136 us
    unnamed x1, local copies, waits for them, and re-layouts  3.13 us

profile of v3, /device:TPU:1, one launch (start us, length us, event | category | flops | bytes accessed | tf_op | source)
XLA Modules:
  0.0 141.5 jit_solution(12779598779701007389)
XLA Ops:
  0.0 0.8 copy.5
  0.8 0.8 copy.6
  1.5 0.1 pad_add_fusion
  1.6 0.6 pad.4.maps
  2.2 136.2 %shard_map.46 = bf16[2,128,4096]{2,1,0:T(8,128)(2,1)} custom-call(bf16[2,128,4096]{2,1,0:T(8,128)(2,1)} %bitcast.7, s32[8,128]{1,0:T(8,128)} %pad.4.maps, bf16[7,512,512]{2,1,0:T(8,128)(2,1)} %inverse.1), custom_call_target="tpu_custom_call" | custom-call | flops 8999999488 | bytes 16000000 | tf_op jit(solution)/shard_map/pallas_call | solution.py:595
  138.4 3.1 %copy.8 = bf16[256,4096]{1,0:T(8,128)(2,1)} copy(bf16[256,4096]{1,0:T(8,128)(2,1)} %bitcast.4) | data formatting | bytes 4194304

commit v4 on v3

--- a/solution.py
+++ b/solution.py
@@ -208,17 +208,23 @@
                         moved = jnp.where(from_cross, src[(other, 0) + part], src[(other, 1) + part])
                         dst[(mine, slot) + part] = (kept.astype(F32) + moved.astype(F32)).astype(BF16)
 
-    def subtract(src, columns_of, dst, factor, slab, rows):
+    def subtract(src, columns_of, dst, factor, slab, rows, count=2):
         width = src.shape[3]
         step = min(width, WIDTH)
-        left = columns_of[slab].reshape(2 * BLOCK, PANEL)
-        keep = lax.broadcasted_iota(jnp.int32, (2 * BLOCK, step), 0) >= rows
+        slabs = pl.ds(slab, count)
+        left = columns_of[slabs].reshape(count * 2 * BLOCK, PANEL)
         for low in range(0, width, step):
             part = pl.ds(low, step)
             product = jnp.dot(left, factor[:, part], preferred_element_type=F32)
-            start = src[slab, :, :, part].reshape(2 * BLOCK, step).astype(F32)
-            reduced = jnp.where(keep, start - product, 0.0).astype(BF16)
-            dst[slab, :, :, part] = reduced.reshape(2, BLOCK, step)
+            start = src[slabs, :, :, part].reshape(count * 2 * BLOCK, step).astype(F32)
+            dst[slabs, :, :, part] = (start - product).astype(BF16).reshape(count, 2, BLOCK, step)
+        for k in range(count):
+            if rows % 16:
+                keep = lax.broadcasted_iota(jnp.int32, (16, width), 0) >= rows
+                top = dst[slab + k, 0, 0:16, :].astype(F32)
+                dst[slab + k, 0, 0:16, :] = jnp.where(keep, top, 0.0).astype(BF16)
+            else:
+                dst[slab + k, 0, 0:rows, :] = jnp.zeros((rows, width), BF16)
 
     def piv0_of(h, f, owner, to):
         slabs = pl.ds(f * 4, 4)
@@ -331,9 +337,7 @@
                 inv[f], piv0[h, pl.ds(f * 4, 4)].reshape(PANEL, HALF), preferred_element_type=F32
             ).astype(BF16)
 
-            @pl.loop(0, 4)
-            def _(j):
-                subtract(parent.at[h], pparent0, front.at[h], upper.at[h, f], f * 4 + j, 32)
+            subtract(parent.at[h], pparent0, front.at[h], upper.at[h, f], f * 4, 32, 4)
 
         @pl.loop(0, 4)
         def _(f):
@@ -359,9 +363,9 @@
                 inv[4 + f], piv1[h, pl.ds(f * 8, 8)].reshape(PANEL, HALF), preferred_element_type=F32
             ).astype(BF16)
 
-            @pl.loop(0, 8)
+            @pl.loop(0, 2)
             def _(j):
-                subtract(parent.at[h], pparent1, front.at[h], upper.at[h, f], f * 8 + j, 16)
+                subtract(parent.at[h], pparent1, front.at[h], upper.at[h, f], f * 8 + j * 4, 16, 4)
 
         others(lambda to: piv1_of(h, r, to).wait_send())
 
@@ -393,12 +397,12 @@
 
         def finish(dy, dx):
             to = at(dy, dx)
-            subtract(parent.at[h], pparent2, front.at[h], upper.at[h, 0], to, 8)
+            subtract(parent.at[h], pparent2, front.at[h], upper.at[h, 0], to, 8, 1)
             out_of(h, g, to).start()
 
         for stage in range(3):
             each_peer(stage, finish)
-        subtract(parent.at[h], pparent2, front.at[h], upper.at[h, 0], g, 8)
+        subtract(parent.at[h], pparent2, front.at[h], upper.at[h, 0], g, 8, 1)
         home(h).start()
 
     def home(h):
@@ -417,6 +421,7 @@
     def _(j):
         ppiv0[j, r] = pparent0[y * 4 + j, 0, 0:32, piece]
 
+    send_child(1, 1)
     inv_copy.wait()
     others(lambda owner: pp0_of(owner, r).wait_recv())
     half0 = pl.ds(multiple(core * 256, 256), 256)
@@ -424,22 +429,20 @@
         inv[y, half0, :], ppiv0[...].reshape(PANEL, BLOCK), preferred_element_type=F32
     ).astype(BF16)
     spread_upper0.begin()
-    send_child(1, 1)
-    send_child(1, 2)
-
     spread_panel.take_passed()
 
     @pl.loop(1, 4)
     def _(i):
         fwd_of((y + i) % 4, core).start()
 
+    spread_upper0.pass_on()
+    send_child(1, 2)
+
     @pl.loop(1, 4)
     def _(i):
         open_panel((y + i) % 4)
 
     own_level0(0)
-    spread_upper0.pass_on()
-    open_stage(1, 0)
 
     spread_upper0.take_direct()
     spread_upper0.take_passed()
@@ -463,9 +466,9 @@
     def _(f):
         up0f_of(f, 1 - core).wait_recv()
 
-        @pl.loop(0, 4)
-        def _(j):
-            subtract(pparent0, pparent0, pfront, pupper0.at[f], f * 4 + j, 32)
+        @pl.loop(0, 2)
+        def _(j):
+            subtract(pparent0, pparent0, pfront, pupper0.at[f], f * 4 + j * 2, 32)
 
     @pl.loop(0, 8)
     def _(j):
@@ -478,8 +481,8 @@
     def _(j):
         ppiv1[j, r] = pparent1[y // 2 * 8 + j, 0, 0:16, piece]
 
+    open_stage(1, 0)
     open_stage(1, 1)
-    open_stage(1, 2)
     own_level1(0)
 
     others(lambda owner: pp1_of(owner, r).wait_recv())
@@ -488,8 +491,9 @@
         inv[4 + y // 2, quarter, :], ppiv1[...].reshape(PANEL, BLOCK), preferred_element_type=F32
     ).astype(BF16)
     spread_upper1.begin()
+    open_stage(1, 2)
+    spread_upper1.pass_on()
     own_level0(1)
-    spread_upper1.pass_on()
     spread_upper1.take_direct()
     spread_upper1.take_passed()
 
@@ -501,9 +505,9 @@
     def _(f):
         up1f_of(f, 1 - core).wait_recv()
 
-        @pl.loop(0, 8)
-        def _(j):
-            subtract(pparent1, pparent1, pfront, pupper1.at[f], f * 8 + j, 16)
+        @pl.loop(0, 4)
+        def _(j):
+            subtract(pparent1, pparent1, pfront, pupper1.at[f], f * 8 + j * 2, 16)
 
     @pl.loop(0, 8)
     def _(j):

time: 142 us -> 133 us (0.937)
  Pallas kernels: 136 us -> 127 us
    pallas_call x1, Pallas kernels: 136 us -> 127 us  [on_device(): result = call(child_front.reshape(2, BLOCK, width), maps, pivot_inverse)]
where the time goes in v4:
time: 133 us
  Pallas kernels  127 us (95%)
  local copies, waits for them, and re-layouts  5.26 us (4%)
    pallas_call x1, Pallas kernels, on_device(): result = call(child_front.reshape(2, BLOCK, width), maps, pivot_inverse)  127 us
    unnamed x1, local copies, waits for them, and re-layouts  3.13 us

profile of v4, /device:TPU:1, one launch (start us, length us, event | category | flops | bytes accessed | tf_op | source)
XLA Modules:
  0.0 132.8 jit_solution(8266528668479876615)
XLA Ops:
  0.0 0.8 copy.5
  0.8 0.8 copy.6
  1.5 0.1 pad_add_fusion
  1.6 0.6 pad.4.maps
  2.2 127.4 %shard_map.46 = bf16[2,128,4096]{2,1,0:T(8,128)(2,1)} custom-call(bf16[2,128,4096]{2,1,0:T(8,128)(2,1)} %bitcast.7, s32[8,128]{1,0:T(8,128)} %pad.4.maps, bf16[7,512,512]{2,1,0:T(8,128)(2,1)} %inverse.1), custom_call_target="tpu_custom_call" | custom-call | flops 8999999488 | bytes 16000000 | tf_op jit(solution)/shard_map/pallas_call | solution.py:599
  129.6 3.1 %copy.8 = bf16[256,4096]{1,0:T(8,128)(2,1)} copy(bf16[256,4096]{1,0:T(8,128)(2,1)} %bitcast.4) | data formatting | bytes 4194304

commit v5 on v4

--- a/solution.py
+++ b/solution.py
@@ -21,7 +21,7 @@
 
 
 def kernel(
-    child, maps, inverse, out,
+    child, own_map, cross_map, inverse, out,
     front, parent, pfront, pparent0, pparent1, pparent2, inv, map_buf, map_tab,
     piv0, piv1, piv2, piv2_wide, ppiv0, ppiv1, upper, pupper0, pupper1,
     map_send, map_recv, a2a_send, a2a_recv, first_send, first_recv,
@@ -93,6 +93,11 @@
             def _(j):
                 self.copy(crossed(0, j), 0, 0, g).wait_recv()
 
+        def take_row(self, dy):
+            @pl.loop(1, 4)
+            def _(i):
+                self.copy(at(dy, i), 0, 0, g).wait_recv()
+
         def take_passed(self):
             @pl.loop(1, 4)
             def _(i):
@@ -115,13 +120,16 @@
     def greet(dy, dx):
         pl.semaphore_signal(barrier, inc=1, device_id=(at(dy, dx) * 4 + r, panel), device_id_type=MESH)
 
-    for stage in range(3):
+    @pl.loop(1, 4)
+    def _(i):
+        pl.semaphore_signal(barrier, inc=1, device_id=(leaf, (panel + i) % 4), device_id_type=MESH)
+
+    for stage in (2, 1, 0):
         each_peer(stage, greet)
 
     @pl.loop(1, 4)
     def _(i):
         pl.semaphore_signal(barrier, inc=1, device_id=(g * 4 + (r + i) % 4, panel), device_id_type=MESH)
-        pl.semaphore_signal(barrier, inc=1, device_id=(leaf, (panel + i) % 4), device_id_type=MESH)
 
     def columns(which, h):
         return pl.ds(multiple(which * WIDTH + h * HALF, HALF), HALF)
@@ -133,8 +141,14 @@
     own_copy(1).start()
     inv_copy = pltpu.make_async_copy(inverse, inv, local_sem.at[1])
     inv_copy.start()
-    map_copy = pltpu.make_async_copy(maps, map_buf.at[g], local_sem.at[2])
-    map_copy.start()
+    row = lax.broadcasted_iota(jnp.int32, (8, 128), 0)
+    lane = lax.broadcasted_iota(jnp.int32, (8, 128), 1)
+    table = jnp.zeros((8, 128), jnp.int32)
+    for level in range(3):
+        for slot in range(2):
+            table = jnp.where((row == level) & (lane == slot), own_map[slot, level], table)
+            table = jnp.where((row == level) & (lane == 2 + slot), cross_map[slot, level], table)
+    map_buf[g] = table
     pl.semaphore_wait(barrier, 21)
 
     def first_copy(half, to_panel, index):
@@ -153,7 +167,7 @@
         first_own.start()
 
     def map_of(slab, to):
-        return remote(maps, map_buf.at[slab], map_send.at[to], map_recv.at[slab], to * 4 + r, panel)
+        return remote(map_buf.at[slab], map_buf.at[slab], map_send.at[to], map_recv.at[slab], to * 4 + r, panel)
 
     def a2a_of(h, slab, to):
         return remote(
@@ -181,7 +195,6 @@
 
     spread_panel.begin()
 
-    map_copy.wait()
 
     def take_map(dy, dx):
         map_of(at(dy, dx), g).wait_recv()
@@ -197,15 +210,18 @@
         step = min(width, WIDTH)
         for mine, other in ((a, b), (b, a)):
             for slot in range(2):
-                from_own = map_tab[mine, level, slot] == 0
-                from_cross = map_tab[mine, level, 2 + slot] == 0
+                own_block = map_tab[mine, level, slot]
+                cross_block = map_tab[mine, level, 2 + slot]
 
                 @pl.loop(0, BLOCK // 32)
                 def _(q):
                     for left in range(0, width, step):
                         part = (pl.ds(multiple(q * 32, 32), 32), pl.ds(left, step))
-                        kept = jnp.where(from_own, src[(mine, 0) + part], src[(mine, 1) + part])
-                        moved = jnp.where(from_cross, src[(other, 0) + part], src[(other, 1) + part])
+                        if level and width == PANEL:
+                            kept, moved = src[(mine, own_block) + part], src[(other, cross_block) + part]
+                        else:
+                            kept = jnp.where(own_block == 0, src[(mine, 0) + part], src[(mine, 1) + part])
+                            moved = jnp.where(cross_block == 0, src[(other, 0) + part], src[(other, 1) + part])
                         dst[(mine, slot) + part] = (kept.astype(F32) + moved.astype(F32)).astype(BF16)
 
     def subtract(src, columns_of, dst, factor, slab, rows, count=2):
@@ -429,10 +445,10 @@
         inv[y, half0, :], ppiv0[...].reshape(PANEL, BLOCK), preferred_element_type=F32
     ).astype(BF16)
     spread_upper0.begin()
-    spread_panel.take_passed()
 
     @pl.loop(1, 4)
     def _(i):
+        spread_panel.take_row(i)
         fwd_of((y + i) % 4, core).start()
 
     spread_upper0.pass_on()
@@ -445,11 +461,12 @@
     own_level0(0)
 
     spread_upper0.take_direct()
-    spread_upper0.take_passed()
-
-    @pl.loop(0, 4)
-    def _(f):
-        up0f_of(f, core).start()
+    up0f_of(y, core).start()
+
+    @pl.loop(1, 4)
+    def _(i):
+        spread_upper0.take_row(i)
+        up0f_of((y + i) % 4, core).start()
 
     @pl.when(panel == 0)
     def _():
@@ -463,12 +480,11 @@
         fwd_of(f, core).wait_send()
 
     @pl.loop(0, 4)
-    def _(f):
+    def _(i):
+        f = (y + i) % 4
         up0f_of(f, 1 - core).wait_recv()
 
-        @pl.loop(0, 2)
-        def _(j):
-            subtract(pparent0, pparent0, pfront, pupper0.at[f], f * 4 + j * 2, 32)
+        subtract(pparent0, pparent0, pfront, pupper0.at[f], f * 4, 32, 4)
 
     @pl.loop(0, 8)
     def _(j):
@@ -505,9 +521,9 @@
     def _(f):
         up1f_of(f, 1 - core).wait_recv()
 
-        @pl.loop(0, 4)
-        def _(j):
-            subtract(pparent1, pparent1, pfront, pupper1.at[f], f * 8 + j * 2, 16)
+        @pl.loop(0, 2)
+        def _(j):
+            subtract(pparent1, pparent1, pfront, pupper1.at[f], f * 8 + j * 4, 16, 4)
 
     @pl.loop(0, 8)
     def _(j):
@@ -552,15 +568,14 @@
 
 def on_device(child_front, own_map, cross_map, pivot_inverse):
     rows, width = child_front.shape
-    maps = jnp.concatenate([own_map[:, 0, :], cross_map[:, 0, :]], axis=1)
-    maps = jnp.pad(maps, ((0, 8 - maps.shape[0]), (0, 128 - maps.shape[1])))
     dma = pltpu.SemaphoreType.DMA
     call = pl.pallas_call(
         kernel,
         out_shape=jax.ShapeDtypeStruct((2, BLOCK, width), BF16),
         in_specs=[
             pl.BlockSpec(memory_space=pl.ANY),
-            pl.BlockSpec(memory_space=pltpu.VMEM),
+            pl.BlockSpec(memory_space=pltpu.SMEM),
+            pl.BlockSpec(memory_space=pltpu.SMEM),
             pl.BlockSpec(memory_space=pl.ANY),
         ],
         out_specs=pl.BlockSpec(memory_space=pl.ANY),
@@ -596,7 +611,8 @@
             flops=9_000_000_000, bytes_accessed=16_000_000, transcendentals=0
         ),
     )
-    result = call(child_front.reshape(2, BLOCK, width), maps, pivot_inverse)
+    tables = [table[:, 0, :].T for table in (own_map, cross_map)]
+    result = call(child_front.reshape(2, BLOCK, width), *tables, pivot_inverse)
     return result.reshape(rows, width)
 
 

time: 133 us -> 129 us (0.970)
  local copies, waits for them, and re-layouts: 5.26 us -> 3.13 us
    pallas_call x1, Pallas kernels: 127 us -> 126 us  [on_device(): result = call(child_front.reshape(2, BLOCK, width), *tables, pivot_inverse)]
    squeeze x2 -> x0, local copies, waits for them, and re-layouts: 1.53 us -> none  [on_device(): maps = jnp.concatenate([own_map[:, 0, :], cross_map[:, 0, :]], axis=1)]
where the time goes in v5:
time: 129 us
  Pallas kernels  126 us (98%)
  local copies, waits for them, and re-layouts  3.13 us (2%)
    pallas_call x1, Pallas kernels, on_device(): result = call(child_front.reshape(2, BLOCK, width), *tables, pivot_inverse)  126 us
    unnamed x1, local copies, waits for them, and re-layouts  3.13 us

profile of v5, /device:TPU:1, one launch (start us, length us, event | category | flops | bytes accessed | tf_op | source)
XLA Modules:
  0.0 128.9 jit_solution(4116292204661462935)
XLA Ops:
  0.0 125.7 %shard_map.46 = bf16[2,128,4096]{2,1,0:T(8,128)(2,1)} custom-call(bf16[2,128,4096]{2,1,0:T(8,128)(2,1)} %bitcast.9, s32[2,3]{1,0:T(2,128)} %bitcast.10, s32[2,3]{1,0:T(2,128)} %bitcast.11, bf16[7,512,512]{2,1,0:T(8,128)(2,1)} %inverse.1), custom_call_target="tpu_custom_call" | custom-call | flops 8999999488 | bytes 16000000 | tf_op jit(solution)/shard_map/pallas_call | solution.py:615
  125.7 3.1 %copy.6 = bf16[256,4096]{1,0:T(8,128)(2,1)} copy(bf16[256,4096]{1,0:T(8,128)(2,1)} %bitcast.8) | data formatting | bytes 4194304

commit v6 on v5

--- a/solution.py
+++ b/solution.py
@@ -22,7 +22,7 @@
 
 def kernel(
     child, own_map, cross_map, inverse, out,
-    front, parent, pfront, pparent0, pparent1, pparent2, inv, map_buf, map_tab,
+    front_a, front_b, parent, pfront, pparent0, pparent1, pparent2, inv, map_buf, map_tab,
     piv0, piv1, piv2, piv2_wide, ppiv0, ppiv1, upper, pupper0, pupper1,
     map_send, map_recv, a2a_send, a2a_recv, first_send, first_recv,
     pan_send, pan_recv, fwd_send, fwd_recv, piv0_send, piv0_recv,
@@ -30,6 +30,7 @@
     pp1_send, pp1_recv, up0_send, up0_recv, up0f_send, up0f_recv,
     up1_send, up1_recv, up1f_send, up1f_recv, out_send, out_recv, local_sem,
 ):
+    fronts = (front_a, front_b)
     leaf = lax.axis_index("leaf")
     panel = lax.axis_index("panel")
     g, r = leaf // 4, leaf % 4
@@ -135,7 +136,7 @@
         return pl.ds(multiple(which * WIDTH + h * HALF, HALF), HALF)
 
     def own_copy(h):
-        return pltpu.make_async_copy(child.at[:, :, columns(g, h)], front.at[h, g], local_sem.at[4 + h])
+        return pltpu.make_async_copy(child.at[:, :, columns(g, h)], fronts[h].at[g], local_sem.at[4 + h])
 
     own_copy(0).start()
     own_copy(1).start()
@@ -171,7 +172,7 @@
 
     def a2a_of(h, slab, to):
         return remote(
-            child.at[:, :, columns(to, h)], front.at[h, slab],
+            child.at[:, :, columns(to, h)], fronts[h].at[slab],
             a2a_send.at[h, to], a2a_recv.at[h, slab], to * 4 + r, panel,
         )
 
@@ -217,7 +218,7 @@
                 def _(q):
                     for left in range(0, width, step):
                         part = (pl.ds(multiple(q * 32, 32), 32), pl.ds(left, step))
-                        if level and width == PANEL:
+                        if level:
                             kept, moved = src[(mine, own_block) + part], src[(other, cross_block) + part]
                         else:
                             kept = jnp.where(own_block == 0, src[(mine, 0) + part], src[(mine, 1) + part])
@@ -256,7 +257,7 @@
     def open_front(h, f):
         @pl.loop(0, 2)
         def _(j):
-            extend(front.at[h], parent.at[h], 0, f * 4 + j, f * 4 + j + 2)
+            extend(fronts[h], parent.at[h], 0, f * 4 + j, f * 4 + j + 2)
 
         @pl.loop(1, 4)
         def _(i):
@@ -335,7 +336,7 @@
 
     def out_of(h, slab, to):
         return remote(
-            front.at[h, to], out.at[:, :, columns(slab, h)],
+            fronts[h].at[to], out.at[:, :, columns(slab, h)],
             out_send.at[h, to], out_recv.at[h, slab], to * 4 + r, panel,
         )
 
@@ -353,7 +354,7 @@
                 inv[f], piv0[h, pl.ds(f * 4, 4)].reshape(PANEL, HALF), preferred_element_type=F32
             ).astype(BF16)
 
-            subtract(parent.at[h], pparent0, front.at[h], upper.at[h, f], f * 4, 32, 4)
+            subtract(parent.at[h], pparent0, fronts[h], upper.at[h, f], f * 4, 32, 4)
 
         @pl.loop(0, 4)
         def _(f):
@@ -362,7 +363,7 @@
         @pl.loop(0, 8)
         def _(j):
             a = j + j // 4 * 4
-            extend(front.at[h], parent.at[h], 1, a, a + 4)
+            extend(fronts[h], parent.at[h], 1, a, a + 4)
 
         others(lambda to: piv1_of(h, r, to).start())
 
@@ -381,13 +382,13 @@
 
             @pl.loop(0, 2)
             def _(j):
-                subtract(parent.at[h], pparent1, front.at[h], upper.at[h, f], f * 8 + j * 4, 16, 4)
+                subtract(parent.at[h], pparent1, fronts[h], upper.at[h, f], f * 8 + j * 4, 16, 4)
 
         others(lambda to: piv1_of(h, r, to).wait_send())
 
         @pl.loop(0, 8)
         def _(j):
-            extend(front.at[h], parent.at[h], 2, j, j + 8)
+            extend(fronts[h], parent.at[h], 2, j, j + 8)
 
         @pl.loop(0, 8)
         def _(j):
@@ -413,16 +414,16 @@
 
         def finish(dy, dx):
             to = at(dy, dx)
-            subtract(parent.at[h], pparent2, front.at[h], upper.at[h, 0], to, 8, 1)
+            subtract(parent.at[h], pparent2, fronts[h], upper.at[h, 0], to, 8, 1)
             out_of(h, g, to).start()
 
         for stage in range(3):
             each_peer(stage, finish)
-        subtract(parent.at[h], pparent2, front.at[h], upper.at[h, 0], g, 8, 1)
+        subtract(parent.at[h], pparent2, fronts[h], upper.at[h, 0], g, 8, 1)
         home(h).start()
 
     def home(h):
-        return pltpu.make_async_copy(front.at[h, g], out.at[:, :, columns(g, h)], local_sem.at[4 + h])
+        return pltpu.make_async_copy(fronts[h].at[g], out.at[:, :, columns(g, h)], local_sem.at[4 + h])
 
     for stage in range(3):
         open_stage(0, stage)
@@ -499,6 +500,7 @@
 
     open_stage(1, 0)
     open_stage(1, 1)
+    open_stage(1, 2)
     own_level1(0)
 
     others(lambda owner: pp1_of(owner, r).wait_recv())
@@ -507,7 +509,6 @@
         inv[4 + y // 2, quarter, :], ppiv1[...].reshape(PANEL, BLOCK), preferred_element_type=F32
     ).astype(BF16)
     spread_upper1.begin()
-    open_stage(1, 2)
     spread_upper1.pass_on()
     own_level0(1)
     spread_upper1.take_direct()
@@ -580,7 +581,8 @@
         ],
         out_specs=pl.BlockSpec(memory_space=pl.ANY),
         scratch_shapes=[
-            pltpu.VMEM((2, 16, 2, BLOCK, HALF), BF16),
+            pltpu.VMEM((16, 2, BLOCK, HALF), BF16),
+            pltpu.VMEM((16, 2, BLOCK, HALF), BF16),
             pltpu.VMEM((2, 16, 2, BLOCK, HALF), BF16),
             pltpu.VMEM((16, 2, BLOCK, PANEL), BF16),
             pltpu.VMEM((16, 2, BLOCK, PANEL), BF16),

time: 129 us -> 127 us (0.984)
  Pallas kernels: 126 us -> 124 us
    pallas_call x1, Pallas kernels: 126 us -> 124 us  [on_device(): result = call(child_front.reshape(2, BLOCK, width), *tables, pivot_inverse)]
where the time goes in v6:
time: 127 us
  Pallas kernels  124 us (98%)
  local copies, waits for them, and re-layouts  3.13 us (2%)
    pallas_call x1, Pallas kernels, on_device(): result = call(child_front.reshape(2, BLOCK, width), *tables, pivot_inverse)  124 us
    unnamed x1, local copies, waits for them, and re-layouts  3.13 us

profile of v6, /device:TPU:1, one launch (start us, length us, event | category | flops | bytes accessed | tf_op | source)
XLA Modules:
  0.0 127.0 jit_solution(14645529350915244505)
XLA Ops:
  0.0 123.9 %shard_map.46 = bf16[2,128,4096]{2,1,0:T(8,128)(2,1)} custom-call(bf16[2,128,4096]{2,1,0:T(8,128)(2,1)} %bitcast.9, s32[2,3]{1,0:T(2,128)} %bitcast.10, s32[2,3]{1,0:T(2,128)} %bitcast.11, bf16[7,512,512]{2,1,0:T(8,128)(2,1)} %inverse.1), custom_call_target="tpu_custom_call" | custom-call | flops 8999999488 | bytes 16000000 | tf_op jit(solution)/shard_map/pallas_call | solution.py:617
  123.9 3.1 %copy.6 = bf16[256,4096]{1,0:T(8,128)(2,1)} copy(bf16[256,4096]{1,0:T(8,128)(2,1)} %bitcast.8) | data formatting | bytes 4194304

commit v7 on v6

--- a/solution.py
+++ b/solution.py
@@ -501,7 +501,6 @@
     open_stage(1, 0)
     open_stage(1, 1)
     open_stage(1, 2)
-    own_level1(0)
 
     others(lambda owner: pp1_of(owner, r).wait_recv())
     quarter = pl.ds(multiple(core * 256 + y % 2 * BLOCK, BLOCK), BLOCK)
@@ -509,6 +508,7 @@
         inv[4 + y // 2, quarter, :], ppiv1[...].reshape(PANEL, BLOCK), preferred_element_type=F32
     ).astype(BF16)
     spread_upper1.begin()
+    own_level1(0)
     spread_upper1.pass_on()
     own_level0(1)
     spread_upper1.take_direct()

time: 127 us -> 127 us (level)
  no operation moved by 1% of the time
where the time goes in v7:
time: 127 us
  Pallas kernels  124 us (98%)
  local copies, waits for them, and re-layouts  3.13 us (2%)
    pallas_call x1, Pallas kernels, on_device(): result = call(child_front.reshape(2, BLOCK, width), *tables, pivot_inverse)  124 us
    unnamed x1, local copies, waits for them, and re-layouts  3.13 us

profile of v7, /device:TPU:1, one launch (start us, length us, event | category | flops | bytes accessed | tf_op | source)
XLA Modules:
  0.0 127.0 jit_solution(3033054381007377769)
XLA Ops:
  0.0 123.9 %shard_map.46 = bf16[2,128,4096]{2,1,0:T(8,128)(2,1)} custom-call(bf16[2,128,4096]{2,1,0:T(8,128)(2,1)} %bitcast.9, s32[2,3]{1,0:T(2,128)} %bitcast.10, s32[2,3]{1,0:T(2,128)} %bitcast.11, bf16[7,512,512]{2,1,0:T(8,128)(2,1)} %inverse.1), custom_call_target="tpu_custom_call" | custom-call | flops 8999999488 | bytes 16000000 | tf_op jit(solution)/shard_map/pallas_call | solution.py:617
  123.9 3.1 %copy.6 = bf16[256,4096]{1,0:T(8,128)(2,1)} copy(bf16[256,4096]{1,0:T(8,128)(2,1)} %bitcast.8) | data formatting | bytes 4194304

commit v8 on v6

--- a/solution.py
+++ b/solution.py
@@ -460,6 +460,8 @@
         open_panel((y + i) % 4)
 
     own_level0(0)
+    open_stage(1, 0)
+    open_stage(1, 1)
 
     spread_upper0.take_direct()
     up0f_of(y, core).start()
@@ -498,8 +500,6 @@
     def _(j):
         ppiv1[j, r] = pparent1[y // 2 * 8 + j, 0, 0:16, piece]
 
-    open_stage(1, 0)
-    open_stage(1, 1)
     open_stage(1, 2)
     own_level1(0)
 

time: 127 us -> 127 us (level)
  no operation moved by 1% of the time
where the time goes in v8:
time: 127 us
  Pallas kernels  124 us (98%)
  local copies, waits for them, and re-layouts  3.13 us (2%)
    pallas_call x1, Pallas kernels, on_device(): result = call(child_front.reshape(2, BLOCK, width), *tables, pivot_inverse)  124 us
    unnamed x1, local copies, waits for them, and re-layouts  3.13 us

profile of v8, /device:TPU:1, one launch (start us, length us, event | category | flops | bytes accessed | tf_op | source)
XLA Modules:
  0.0 127.2 jit_solution(14130663565647142140)
XLA Ops:
  0.0 124.0 %shard_map.46 = bf16[2,128,4096]{2,1,0:T(8,128)(2,1)} custom-call(bf16[2,128,4096]{2,1,0:T(8,128)(2,1)} %bitcast.9, s32[2,3]{1,0:T(2,128)} %bitcast.10, s32[2,3]{1,0:T(2,128)} %bitcast.11, bf16[7,512,512]{2,1,0:T(8,128)(2,1)} %inverse.1), custom_call_target="tpu_custom_call" | custom-call | flops 8999999488 | bytes 16000000 | tf_op jit(solution)/shard_map/pallas_call | solution.py:617
  124.0 3.1 %copy.6 = bf16[256,4096]{1,0:T(8,128)(2,1)} copy(bf16[256,4096]{1,0:T(8,128)(2,1)} %bitcast.8) | data formatting | bytes 4194304
